TPU v7x, 32 devices: a whole 2x2x4 slice. The times are simulated.
32 devices in a mesh: shard: 8 (over z, core), ctx: 2 (over x), tp: 2 (over y).
Axes of the slice: x: 2, y: 2, z: 4, core: 2. Of those that a mesh axis runs over, the one named last changes fastest.
Arguments:
- tokens: bfloat16 [16, 2048, 1024], P('shard', 'ctx'), may hold values from -6 to 6
- cotangent: bfloat16 [16, 2048, 1024], P('shard', 'ctx'), may hold values from -6 to 6
- adapter_pick: int32 [16], P('shard'), may hold values from 0 to 7
- positions: int32 [3, 16, 2048], P(None, 'shard', 'ctx'), may hold values from 0 to 15
- first_gain: float32 [1024], replicated, may hold values from 0.1 to 1.9
- first_shift: float32 [1024], replicated, may hold values from -3 to 3
- joined_weight: bfloat16 [1024, 3, 1024], P('shard', None, 'tp'), may hold values from -0.1875 to 0.1875
- joined_bias: float32 [3, 1024], P(None, 'tp'), may hold values from -3 to 3
- output_weight: bfloat16 [1024, 1024], P('tp', 'shard'), may hold values from -0.75 to 0.75
- mixing_exit_offset: float32 [1024], replicated, may hold values from -3 to 3
- second_gain: float32 [1024], replicated, may hold values from 0.1 to 1.9
- second_shift: float32 [1024], replicated, may hold values from -3 to 3
- expand_weight: bfloat16 [1024, 4096], P('shard', 'tp'), may hold values from -0.1875 to 0.1875
- widening_offset: float32 [4096], P('tp'), may hold values from -3 to 3
- reduce_weight: bfloat16 [4096, 1024], P('tp', 'shard'), may hold values from -0.09375 to 0.09375
- shrinking_offset: float32 [1024], replicated, may hold values from -3 to 3
- joined_down: bfloat16 [8, 1024, 16], replicated, may hold values from -0.1875 to 0.1875
- joined_up: bfloat16 [8, 16, 3, 1024], P(None, None, None, 'tp'), may hold values from -1.5 to 1.5
- output_down: bfloat16 [8, 1024, 16], P(None, 'tp'), may hold values from -0.75 to 0.75
- output_up: bfloat16 [8, 16, 1024], replicated, may hold values from -1.5 to 1.5
- expand_down: bfloat16 [8, 1024, 16], replicated, may hold values from -0.1875 to 0.1875
- expand_up: bfloat16 [8, 16, 4096], P(None, None, 'tp'), may hold values from -1.5 to 1.5
- reduce_down: bfloat16 [8, 4096, 16], P(None, 'tp'), may hold values from -0.09375 to 0.09375
- reduce_up: bfloat16 [8, 16, 1024], replicated, may hold values from -1.5 to 1.5
Outputs:
- output: bfloat16 [16, 2048, 1024], P('shard', 'ctx')
- tokens_grad: bfloat16 [16, 2048, 1024], P('shard', ('ctx', 'tp'))
- joined_down_grad: float32 [8, 1024, 16], replicated
- joined_up_grad: float32 [8, 16, 3, 1024], P(None, None, None, 'tp')
- output_down_grad: float32 [8, 1024, 16], P(None, 'tp')
- output_up_grad: float32 [8, 16, 1024], replicated
- expand_down_grad: float32 [8, 1024, 16], replicated
- expand_up_grad: float32 [8, 16, 4096], P(None, None, 'tp')
- reduce_down_grad: float32 [8, 4096, 16], P(None, 'tp')
- reduce_up_grad: float32 [8, 16, 1024], replicated
Inputs may be any that keep to these rules, and one draw needn't show every extreme that they name: `positions`: integer places on a grid of 16 frames by 16 by 16 patches.
All inputs are finite; a program needn't handle non-finite values.
Results may differ from a plain program's by a relative error of at most 0.022.
The roundings to bfloat16 on the way count: a program that leaves them out, or rounds other values in their place, can miss the bound.
Values may be sent and summed in bfloat16 or wider, within the bound.
A program may use at most 448 MiB of HBM per device.

v0:
```python
import math

import jax
import jax.numpy as jnp
from jax import lax
from jax.sharding import PartitionSpec as P

eps_norm = 1e-06
score_scale = 0.125


def rope_tables(places):
    band = jnp.arange(10, dtype=jnp.float32)
    rates = jnp.exp(band * (-math.log(10000.0) / 10.0))
    angle = places.astype(jnp.float32)[..., None] * rates
    cos_parts = []
    sin_parts = []
    for band_index in range(3):
        cosine = jnp.cos(angle[band_index])
        sine = jnp.sin(angle[band_index])
        cos_parts = cos_parts + [cosine, cosine]
        sin_parts = sin_parts + [-sine, sine]
    rest_shape = angle.shape[1:-1] + (4,)
    cos_parts.append(jnp.ones(rest_shape, jnp.float32))
    sin_parts.append(jnp.zeros(rest_shape, jnp.float32))
    return (jnp.concatenate(cos_parts, -1), jnp.concatenate(sin_parts, -1))


def swap_pairs(values):
    leading = values.shape[:-1]
    turned = values[..., :60].reshape(leading + (3, 2, 10))[..., ::-1, :].reshape(leading + (60,))
    return jnp.concatenate([turned, values[..., 60:]], -1)


def rotate(values, cosine, sine):
    return values * cosine[..., None, :] + swap_pairs(values) * sine[..., None, :]


def rotate_back(grads, cosine, sine):
    return grads * cosine[..., None, :] + swap_pairs(grads * sine[..., None, :])


def norm_forward(values, gain, shift):
    centred = values - jnp.mean(values, -1, keepdims=True)
    inverse = lax.rsqrt(jnp.mean(centred * centred, -1, keepdims=True) + eps_norm)
    scaled = centred * inverse
    return (scaled * gain + shift, scaled, inverse)


def norm_back(grads, scaled, inverse, gain):
    weighted = grads * gain
    return inverse * (
        weighted
        - jnp.mean(weighted, -1, keepdims=True)
        - scaled * jnp.mean(weighted * scaled, -1, keepdims=True)
    )


def select_factor(choose, table):
    return jnp.einsum("ca,a...->c...", choose, table, preferred_element_type=jnp.float32).astype(
        jnp.bfloat16
    )


def gelu_exact(values):
    return jax.nn.gelu(values, approximate=False)


def matrix_product(form, left, right):
    return jnp.einsum(form, left, right, preferred_element_type=jnp.float32)


def shards(
    tokens,
    cotangent,
    adapter_pick,
    positions,
    first_gain,
    first_shift,
    joined_weight,
    joined_bias,
    output_weight,
    mixing_exit_offset,
    second_gain,
    second_shift,
    expand_weight,
    widening_offset,
    reduce_weight,
    shrinking_offset,
    joined_down,
    joined_up,
    output_down,
    output_up,
    expand_down,
    expand_up,
    reduce_down,
    reduce_up,
):
    whole_joined, whole_output, whole_expand, whole_reduce = (
        lax.all_gather(joined_weight, "shard", axis=0, tiled=True),
        lax.all_gather(output_weight, "shard", axis=1, tiled=True),
        lax.all_gather(expand_weight, "shard", axis=0, tiled=True),
        lax.all_gather(reduce_weight, "shard", axis=1, tiled=True),
    )
    clip_count, local_len, width = tokens.shape
    local_width = whole_joined.shape[2]
    head_count = local_width // 64
    choose = (
        adapter_pick[:, None] == jnp.arange(joined_down.shape[0], dtype=jnp.int32)[None, :]
    ).astype(jnp.bfloat16)
    select_joined_down = select_factor(choose, joined_down)
    select_joined_up = select_factor(choose, joined_up)
    select_output_down = select_factor(choose, output_down)
    select_output_up = select_factor(choose, output_up)
    select_expand_down = select_factor(choose, expand_down)
    select_expand_up = select_factor(choose, expand_up)
    select_reduce_down = select_factor(choose, reduce_down)
    select_reduce_up = select_factor(choose, reduce_up)
    cosine, sine = rope_tables(positions)
    block_arguments = tokens.astype(jnp.float32)
    norm_one, scaled_one, inverse_one = norm_forward(block_arguments, first_gain, first_shift)
    initial_standardized = norm_one.astype(jnp.bfloat16)
    initial_slim_derivative = matrix_product(
        "zgh,zhe->zge", initial_standardized, select_joined_down
    ).astype(jnp.bfloat16)
    mapped_vectors = (
        matrix_product("cld,dje->clje", initial_standardized, whole_joined)
        + joined_bias
        + matrix_product("uip,upqg->uiqg", initial_slim_derivative, select_joined_up)
    )
    head_shape = (clip_count, local_len, head_count, 64)
    query = rotate(mapped_vectors[:, :, 0].reshape(head_shape), cosine, sine).astype(jnp.bfloat16)
    keys = rotate(mapped_vectors[:, :, 1].reshape(head_shape), cosine, sine).astype(jnp.bfloat16)
    values = mapped_vectors[:, :, 2].reshape(head_shape).astype(jnp.bfloat16)
    stats_shape = (clip_count, head_count, local_len)
    run_max = jnp.full(stats_shape, -1e30, jnp.float32)
    key_part = lax.all_gather(keys, "ctx", axis=1, tiled=True)
    value_part = lax.all_gather(values, "ctx", axis=1, tiled=True)
    scores = matrix_product("cqhd,ckhd->chqk", query, key_part) * score_scale
    new_max = jnp.maximum(run_max, jnp.max(scores, -1))
    weights = jnp.exp(scores - new_max[..., None])
    run_total = jnp.sum(weights, -1)
    update = matrix_product("chqk,ckhd->cqhd", weights.astype(jnp.bfloat16), value_part)
    accum = update
    run_max, run_total, accum = (new_max, run_total, accum)
    log_total = run_max + jnp.log(run_total)
    attended_full = accum / jnp.transpose(run_total, (0, 2, 1))[..., None]
    mixing_outcome = attended_full.reshape(clip_count, local_len, local_width).astype(jnp.bfloat16)
    out_part = matrix_product("cle,ed->cld", mixing_outcome, whole_output)
    rank_partial = matrix_product("fig,fgt->fit", mixing_outcome, select_output_down)
    output_total, rank_sum = (
        lax.psum(out_part.astype(jnp.bfloat16), "tp").astype(jnp.float32),
        lax.psum(rank_partial.astype(jnp.bfloat16), "tp").astype(jnp.float32),
    )
    middle_slim_derivative = rank_sum.astype(jnp.bfloat16)
    first_hidden = (
        block_arguments
        + output_total
        + mixing_exit_offset
        + matrix_product("wnk,wke->wne", middle_slim_derivative, select_output_up)
    )
    norm_two, scaled_two, inverse_two = norm_forward(first_hidden, second_gain, second_shift)
    latter_standardized = norm_two.astype(jnp.bfloat16)
    penultimate_slim_derivative = matrix_product(
        "zgh,zhe->zge", latter_standardized, select_expand_down
    ).astype(jnp.bfloat16)
    skip_stream_vectors = (
        matrix_product("cld,df->clf", latter_standardized, whole_expand)
        + widening_offset
        + matrix_product("uqz,uze->uqe", penultimate_slim_derivative, select_expand_up)
    )
    activity, gelu_pull = jax.vjp(gelu_exact, skip_stream_vectors)
    gaussian_error_unit = activity.astype(jnp.bfloat16)
    mlp_part = matrix_product("clf,fd->cld", gaussian_error_unit, whole_reduce)
    fourth_rank_partial = matrix_product("xpv,xvy->xpy", gaussian_error_unit, select_reduce_down)
    feedforward_sum, rank_four_sum = (
        lax.psum(mlp_part.astype(jnp.bfloat16), "tp").astype(jnp.float32),
        lax.psum(fourth_rank_partial.astype(jnp.bfloat16), "tp").astype(jnp.float32),
    )
    closing_slim_derivative = rank_four_sum.astype(jnp.bfloat16)
    output = (
        first_hidden
        + feedforward_sum
        + shrinking_offset
        + matrix_product("wnk,wke->wne", closing_slim_derivative, select_reduce_up)
    ).astype(jnp.bfloat16)
    back_joined, back_output, back_expand, back_reduce = (
        lax.all_gather(joined_weight, "shard", axis=0, tiled=True),
        lax.all_gather(output_weight, "shard", axis=1, tiled=True),
        lax.all_gather(expand_weight, "shard", axis=0, tiled=True),
        lax.all_gather(reduce_weight, "shard", axis=1, tiled=True),
    )
    reduce_up_term = matrix_product("vkn,vkm->vnm", closing_slim_derivative, cotangent)
    gradient_fourth = matrix_product("abj,awj->abw", cotangent, select_reduce_up).astype(
        jnp.bfloat16
    )
    reduce_down_term = matrix_product("mpg,mpu->mgu", gaussian_error_unit, gradient_fourth)
    grad_active = matrix_product("cld,fd->clf", cotangent, back_reduce) + matrix_product(
        "gez,guz->geu", gradient_fourth, select_reduce_down
    )
    residual_gradient = gelu_pull(grad_active)[0].astype(jnp.bfloat16)
    expand_up_term = matrix_product("jge,jgn->jen", penultimate_slim_derivative, residual_gradient)
    grad_norm_part = matrix_product("clf,df->cld", residual_gradient, back_expand)
    third_gradient_part = matrix_product("aik,adk->aid", residual_gradient, select_expand_up)
    norm_gradient_sum, grad_three_sum = (
        lax.psum(grad_norm_part.astype(jnp.bfloat16), "tp").astype(jnp.float32),
        lax.psum(third_gradient_part.astype(jnp.bfloat16), "tp").astype(jnp.float32),
    )
    gradient_third = grad_three_sum.astype(jnp.bfloat16)
    expand_down_term = matrix_product("kgt,kgh->kth", latter_standardized, gradient_third)
    second_norm_gradient = norm_gradient_sum + matrix_product(
        "jqt,jit->jqi", gradient_third, select_expand_down
    )
    grad_hidden = cotangent.astype(jnp.float32) + norm_back(
        second_norm_gradient, scaled_two, inverse_two, second_gain
    )
    branch_gradient = grad_hidden.astype(jnp.bfloat16)
    output_up_term = matrix_product("vkn,vkm->vnm", middle_slim_derivative, branch_gradient)
    gradient_second = matrix_product("abj,awj->abw", branch_gradient, select_output_up).astype(
        jnp.bfloat16
    )
    output_down_term = matrix_product("nua,nui->nai", mixing_outcome, gradient_second)
    grad_attended = (
        (
            matrix_product("cld,ed->cle", branch_gradient, back_output)
            + matrix_product("gsq,ghq->gsh", gradient_second, select_output_down)
        )
        .astype(jnp.bfloat16)
        .reshape(head_shape)
    )
    key_whole, value_whole = (
        lax.all_gather(keys, "ctx", axis=1, tiled=True),
        lax.all_gather(values, "ctx", axis=1, tiled=True),
    )
    flat_shape = (clip_count, local_len, local_width)

    def clip_back(items):
        query_clip, key_clip, value_clip, grad_clip, total_clip = items
        scores = matrix_product("qhd,khd->hqk", query_clip, key_clip) * score_scale
        probs = jnp.exp(scores - total_clip[..., None])
        grad_probs = matrix_product("qhd,khd->hqk", grad_clip, value_clip)
        middle = jnp.sum(probs * grad_probs, -1, keepdims=True)
        grad_scores = (probs * (grad_probs - middle)).astype(jnp.bfloat16)
        grad_query = matrix_product("hqk,khd->qhd", grad_scores, key_clip) * score_scale
        grad_key = matrix_product("hqk,qhd->khd", grad_scores, query_clip) * score_scale
        grad_value = matrix_product("hqk,qhd->khd", probs.astype(jnp.bfloat16), grad_clip)
        return (grad_query, grad_key, grad_value)

    grad_query, key_terms, value_terms = lax.map(
        clip_back, (query, key_whole, value_whole, grad_attended, log_total)
    )
    full_len = key_whole.shape[1]
    key_sum, value_sum = (
        lax.psum_scatter(
            key_terms.reshape(clip_count, full_len, local_width).astype(jnp.bfloat16),
            "ctx",
            scatter_dimension=1,
            tiled=True,
        ).astype(jnp.float32),
        lax.psum_scatter(
            value_terms.reshape(clip_count, full_len, local_width).astype(jnp.bfloat16),
            "ctx",
            scatter_dimension=1,
            tiled=True,
        ).astype(jnp.float32),
    )
    query_key_value_gradient = jnp.stack(
        [
            rotate_back(grad_query, cosine, sine).reshape(flat_shape),
            rotate_back(key_sum.reshape(head_shape), cosine, sine).reshape(flat_shape),
            value_sum,
        ],
        axis=2,
    ).astype(jnp.bfloat16)
    joined_up_term = matrix_product(
        "pvh,pvfo->phfo", initial_slim_derivative, query_key_value_gradient
    )
    first_gradient_part = matrix_product(
        "kxsd,ktsd->kxt", query_key_value_gradient, select_joined_up
    )
    grad_norm_one_part = matrix_product("clje,dje->cld", query_key_value_gradient, back_joined)
    gradient_first = lax.psum(first_gradient_part.astype(jnp.bfloat16), "tp")
    grad_norm_share = lax.psum_scatter(
        grad_norm_one_part.astype(jnp.bfloat16), "tp", scatter_dimension=1, tiled=True
    ).astype(jnp.float32)
    joined_down_term = matrix_product("kgt,kgh->kth", initial_standardized, gradient_first)
    half_len = grad_norm_share.shape[1]
    begin = lax.axis_index("tp") * half_len

    def shared_rows(array):
        return lax.dynamic_slice_in_dim(array, begin, half_len, 1)

    grad_norm_one = grad_norm_share + matrix_product(
        "jqt,jit->jqi", shared_rows(gradient_first), select_joined_down
    )
    tokens_grad = (
        shared_rows(grad_hidden)
        + norm_back(grad_norm_one, shared_rows(scaled_one), shared_rows(inverse_one), first_gain)
    ).astype(jnp.bfloat16)
    choose_full = choose.astype(jnp.float32)

    def by_adapter(term):
        return jnp.einsum(
            "ca,c...->a...",
            choose_full,
            term,
            precision=lax.Precision.HIGHEST,
            preferred_element_type=jnp.float32,
        )

    summed = lax.psum(
        (
            by_adapter(joined_down_term),
            by_adapter(joined_up_term),
            by_adapter(output_down_term),
            by_adapter(output_up_term),
            by_adapter(expand_down_term),
            by_adapter(expand_up_term),
            by_adapter(reduce_down_term),
            by_adapter(reduce_up_term),
        ),
        ("shard", "ctx"),
    )
    return (
        output,
        tokens_grad,
        summed[0],
        summed[1],
        summed[2],
        summed[3],
        summed[4],
        summed[5],
        summed[6],
        summed[7],
    )


def solution(mesh):
    return jax.shard_map(
        shards,
        mesh=mesh,
        in_specs=(
            P("shard", "ctx", None),
            P("shard", "ctx", None),
            P("shard"),
            P(None, "shard", "ctx"),
            P(),
            P(),
            P("shard", None, "tp"),
            P(None, "tp"),
            P("tp", "shard"),
            P(),
            P(),
            P(),
            P("shard", "tp"),
            P("tp"),
            P("tp", "shard"),
            P(),
            P(),
            P(None, None, None, "tp"),
            P(None, "tp", None),
            P(),
            P(),
            P(None, None, "tp"),
            P(None, "tp", None),
            P(),
        ),
        out_specs=(
            P("shard", "ctx", None),
            P("shard", ("ctx", "tp"), None),
            P(),
            P(None, None, None, "tp"),
            P(None, "tp", None),
            P(),
            P(),
            P(None, None, "tp"),
            P(None, "tp", None),
            P(),
        ),
        check_vma=False,
    )
```

profile of v0, /device:TPU:0, one launch (start us, length us, event | category | flops | bytes accessed | tf_op | source)
XLA Modules:
  0.0 1509.1 jit_solution(10445737411258771576)
XLA Ops:
  118.3 49.0 %all-gather.11.cloned.1.call-done = bf16[2,2048,8,64]{1,3,2,0:T(8,128)(2,1)} async-done(((bf16[2,1024,8,64]{1,3,2,0:T(8,128)(2,1)}), bf16[2,2048,8,64]{1,3,2,0:T(8,128)(2,1)}) %all-gather.11.cloned.1.call-update) | async-done | bytes 4194320 | tf_op jit(solution)/shard_map/all_gather | solution.py:137
  167.4 47.6 %multiply_reduce_fusion.1 = (f32[2,8,1024]{2,1,0:T(8,128)S(1)}, f32[2,8,1024,2048]{3,2,1,0:T(8,128)}) fusion(bf16[2,1024,8,64]{1,3,2,0:T(8,128)(2,1)S(1)} %get-tuple-element.213, bf16[2,2048,8,64]{1,3,2,0:T(8,128)(2,1)} %all-gather.11.cloned.1.call-done), kind=kOutput, calls=%fused_computation.33 | convolution fusion | flops 4362059776 | bytes 140574720 | tf_op jit(solution)/shard_map/cqhd,ckhd->chqk/dot_general | solution.py:70
  215.6 41.0 %fusion.30 = f32[2,8,1024]{2,1,0:T(8,128)S(1)} fusion(f32[2,8,1024,2048]{3,2,1,0:T(8,128)} %get-tuple-element.141, f32[2,8,1024]{2,1,0:T(8,128)S(1)} %broadcast_maximum_fusion), kind=kLoop, calls=%fused_computation.34 | loop fusion | flops 100646912 | bytes 134348800 | tf_op jit(solution)/shard_map/reduce_sum | solution.py:142
  256.7 45.4 %fusion.59 = bf16[2,1024,8,64]{1,3,2,0:T(8,128)(2,1)S(1)} fusion(bf16[2,2048,8,64]{1,3,2,0:T(8,128)(2,1)} %all-gather.9.cloned.1.call-done, f32[2,8,1024,2048]{3,2,1,0:T(8,128)} %get-tuple-element.141, f32[2,8,1024]{2,1,0:T(8,128)S(1)} %broadcast_maximum_fusion, f32[2,1024,8]{1,2,0:T(8,128)S(1)} %bitcast.259), kind=kOutput, calls=%fused_computation.98 | convolution fusion | flops 4397727744 | bytes 140640256 | tf_op jit(solution)/shard_map/chqk,ckhd->cqhd/dot_general | solution.py:70
  333.8 85.3 %all-reduce.15.cloned.1.call-done = (bf16[2,1024,1024]{2,1,0:T(8,128)(2,1)}, bf16[2,1024,16]{1,2,0:T(8,128)(2,1)}) async-done(((bf16[2,1024,1024]{2,1,0:T(8,128)(2,1)}, bf16[2,1024,16]{1,2,0:T(8,128)(2,1)}), (bf16[2,1024,1024]{2,1,0:T(8,128)(2,1)}, bf16[2,1024,16]{1,2,0:T(8,128)(2,1)})) %all-reduce.15.cloned.1.call-update) | async-done | bytes 4259856 | tf_op jit(solution)/shard_map/psum | solution.py:152
  431.0 36.9 %all-gather.15.cloned.1.call-done = bf16[1024,2048]{1,0:T(8,128)(2,1)} async-done(((bf16[128,2048]{1,0:T(8,128)(2,1)}), bf16[1024,2048]{1,0:T(8,128)(2,1)}) %all-gather.15.cloned.1.call-update) | async-done | bytes 4194320 | tf_op jit(solution)/shard_map/all_gather | solution.py:102
  500.6 41.0 %multiply_convert_fusion.1 = (bf16[2,1024,2048]{2,1,0:T(8,128)(2,1)}, f32[2,1024,2048]{2,1,0:T(8,128)}) fusion(f32[2,1024,2048]{2,1,0:T(8,128)} %get-tuple-element.144, u8[1024,2048]{1,0:T(8,128)(4,1)} %get-tuple-element.83, u8[1024,2048]{1,0:T(8,128)(4,1)S(1)} %get-tuple-element.82), kind=kLoop, calls=%fused_computation.45 | loop fusion | flops 293601280 | bytes 46137344 | tf_op jit(solution)/shard_map/convert_element_type | solution.py:173
  541.7 17.7 %add_convert_fusion = bf16[2,1024,2048]{2,1,0:T(8,128)(2,1)S(1)} fusion(f32[2,1024,2048]{2,1,0:T(8,128)} %get-tuple-element.122, f32[2,1024,2048]{2,1,0:T(8,128)} %fusion.51, f32[2,1024,2048]{2,1,0:T(8,128)} %get-tuple-element.144, bf16[2,16,1024]{2,1,0:T(8,128)(2,1)S(1)} %convolution_convert_fusion.7, bf16[2,2048,16]{1,0,2:T(2,128)(2,1)S(1)} %convolution_convert_fusion.1), kind=kOutput, calls=%fused_computation.44 | convolution fusion | flops 197132288 | bytes 58916864 | tf_op jit(solution)/shard_map/gez,guz->geu/dot_general | solution.py:70
  575.7 108.4 %all-reduce.13.cloned.1.call-done = (bf16[2,1024,1024]{2,1,0:T(8,128)(2,1)}, bf16[2,1024,16]{1,2,0:T(8,128)(2,1)}) async-done(((bf16[2,1024,1024]{2,1,0:T(8,128)(2,1)}, bf16[2,1024,16]{1,2,0:T(8,128)(2,1)}), (bf16[2,1024,1024]{2,1,0:T(8,128)(2,1)}, bf16[2,1024,16]{1,2,0:T(8,128)(2,1)})) %all-reduce.13.cloned.1.call-update) | async-done | bytes 4259856 | tf_op jit(solution)/shard_map/psum | solution.py:206
  702.4 363.0 %while.14 = (s32[]{:T(128)}, f32[2,1024,8,64]{1,3,2,0:T(8,128)}, bf16[2,2048,8,64]{1,3,2,0:T(8,128)(2,1)}, bf16[2,2048,8,64]{1,3,2,0:T(8,128)(2,1)}, bf16[2,2048...) while((s32[]{:T(128)}, f32[2,1024,8,64]{1,3,2,0:T(8,128)}, ...), condition=%wide.region_16.17_spmd, body=%wide.region_14.16_spmd.sunk | while | flops 10940309504 | bytes 549688448 | solution.py:249
  702.8 24.9 %fusion.225 = f32[8,1024,2048]{2,1,0:T(8,128)} fusion(bf16[2,2048,8,64]{1,3,2,0:T(8,128)(2,1)} %get-tuple-element.232, s32[]{:T(128)} %get-tuple-element.218, bf16[2,1024,8,64]{1,3,2,0:T(8,128)(2,1)S(1)} %get-tuple-element.233), kind=kOutput, calls=%fused_computation.12.clone.1 | convolution fusion | flops 2147483648 | bytes 70255616 | tf_op jit(solution)/shard_map/while/body/eval_jaxpr/qhd,khd->hqk/dot_general | solution.py:70
  727.7 44.9 %multiply_reduce_fusion.6 = (f32[8,1024]{1,0:T(8,128)S(1)}, f32[8,1024,2048]{2,1,0:T(8,128)}) fusion(f32[8,1024,2048]{2,1,0:T(8,128)} %fusion.225, f32[8,1024]{1,0:T(8,128)S(1)} %dynamic-slice_bitcast_fusion.2, bf16[2,2048,8,64]{1,3,2,0:T(8,128)(2,1)S(1)} %copy-done.9, s32[]{:T(128)} %get-tuple-element.218, bf16[2,1024,8,64]{1,3,2,0:T(8,128)(2,1)S(1)} %copy-done.6), kind=kOutput, calls=%fused_computation.1.clone.3 | convolution fusion | flops 2214584320 | bytes 137430016 | tf_op jit(solution)/shard_map/while/body/eval_jaxpr/qhd,khd->hqk/dot_general | solution.py:70
  772.5 53.0 %multiply_convert_fusion.3 = bf16[8,1024,2048]{2,1,0:T(8,128)(2,1)} fusion(f32[8,1024,2048]{2,1,0:T(8,128)} %get-tuple-element.206, f32[8,1024,2048]{2,1,0:T(8,128)} %fusion.225, f32[8,1024]{1,0:T(8,128)S(1)} %get-tuple-element.207, f32[8,1024]{1,0:T(8,128)S(1)} %dynamic-slice_bitcast_fusion.2), kind=kLoop, calls=%fused_computation.clone.1 | loop fusion | flops 83886080 | bytes 167837696 | tf_op jit(solution)/shard_map/while/body/eval_jaxpr/convert_element_type | solution.py:243
  840.7 18.0 %bitcast_dynamic-update-slice_fusion.6 = f32[2,1024,8,64]{1,3,2,0:T(8,128)} fusion(f32[2,1024,8,64]{1,3,2,0:T(8,128)} %get-tuple-element.219, s32[]{:T(128)} %get-tuple-element.218, bf16[8,1024,2048]{2,1,0:T(8,128)(2,1)} %multiply_convert_fusion.3, bf16[2,2048,8,64]{1,3,2,0:T(8,128)(2,1)} %get-tuple-element.232), kind=kOutput, calls=%fused_computation.7.clone.1 | convolution fusion | flops 2148007936 | bytes 37749760 | tf_op jit(solution)/shard_map/while/body/eval_jaxpr/hqk,khd->qhd/dot_general | solution.py:70
  858.7 25.3 %bitcast_dynamic-update-slice_fusion.8 = bf16[2,2048,8,64]{1,3,2,0:T(8,128)(2,1)} fusion(bf16[2,2048,8,64]{1,3,2,0:T(8,128)(2,1)} %get-tuple-element.221, s32[]{:T(128)} %get-tuple-element.218, f32[8,1024,2048]{2,1,0:T(8,128)} %fusion.225, f32[8,1024]{1,0:T(8,128)S(1)} %dynamic-slice_bitcast_fusion.2, bf16[2,1024,8,64]{1,3,2,0:T(8,128)(2,1)} %get-tuple-element.235), kind=kOutput, calls=%fused_computation.5.clone.1 | convolution fusion | flops 2197815296 | bytes 72385536 | tf_op jit(solution)/shard_map/while/body/eval_jaxpr/hqk,qhd->khd/dot_general | solution.py:70
  884.0 24.9 %fusion.225 = f32[8,1024,2048]{2,1,0:T(8,128)} fusion(bf16[2,2048,8,64]{1,3,2,0:T(8,128)(2,1)} %get-tuple-element.232, s32[]{:T(128)} %get-tuple-element.218, bf16[2,1024,8,64]{1,3,2,0:T(8,128)(2,1)S(1)} %get-tuple-element.233), kind=kOutput, calls=%fused_computation.12.clone.1 | convolution fusion | flops 2147483648 | bytes 70255616 | tf_op jit(solution)/shard_map/while/body/eval_jaxpr/qhd,khd->hqk/dot_general | solution.py:70
  908.9 44.9 %multiply_reduce_fusion.6 = (f32[8,1024]{1,0:T(8,128)S(1)}, f32[8,1024,2048]{2,1,0:T(8,128)}) fusion(f32[8,1024,2048]{2,1,0:T(8,128)} %fusion.225, f32[8,1024]{1,0:T(8,128)S(1)} %dynamic-slice_bitcast_fusion.2, bf16[2,2048,8,64]{1,3,2,0:T(8,128)(2,1)S(1)} %copy-done.9, s32[]{:T(128)} %get-tuple-element.218, bf16[2,1024,8,64]{1,3,2,0:T(8,128)(2,1)S(1)} %copy-done.6), kind=kOutput, calls=%fused_computation.1.clone.3 | convolution fusion | flops 2214584320 | bytes 137430016 | tf_op jit(solution)/shard_map/while/body/eval_jaxpr/qhd,khd->hqk/dot_general | solution.py:70
  953.7 53.0 %multiply_convert_fusion.3 = bf16[8,1024,2048]{2,1,0:T(8,128)(2,1)} fusion(f32[8,1024,2048]{2,1,0:T(8,128)} %get-tuple-element.206, f32[8,1024,2048]{2,1,0:T(8,128)} %fusion.225, f32[8,1024]{1,0:T(8,128)S(1)} %get-tuple-element.207, f32[8,1024]{1,0:T(8,128)S(1)} %dynamic-slice_bitcast_fusion.2), kind=kLoop, calls=%fused_computation.clone.1 | loop fusion | flops 83886080 | bytes 167837696 | tf_op jit(solution)/shard_map/while/body/eval_jaxpr/convert_element_type | solution.py:243
  1021.9 18.0 %bitcast_dynamic-update-slice_fusion.6 = f32[2,1024,8,64]{1,3,2,0:T(8,128)} fusion(f32[2,1024,8,64]{1,3,2,0:T(8,128)} %get-tuple-element.219, s32[]{:T(128)} %get-tuple-element.218, bf16[8,1024,2048]{2,1,0:T(8,128)(2,1)} %multiply_convert_fusion.3, bf16[2,2048,8,64]{1,3,2,0:T(8,128)(2,1)} %get-tuple-element.232), kind=kOutput, calls=%fused_computation.7.clone.1 | convolution fusion | flops 2148007936 | bytes 37749760 | tf_op jit(solution)/shard_map/while/body/eval_jaxpr/hqk,khd->qhd/dot_general | solution.py:70
  1039.9 25.4 %bitcast_dynamic-update-slice_fusion.8 = bf16[2,2048,8,64]{1,3,2,0:T(8,128)(2,1)} fusion(bf16[2,2048,8,64]{1,3,2,0:T(8,128)(2,1)} %get-tuple-element.221, s32[]{:T(128)} %get-tuple-element.218, f32[8,1024,2048]{2,1,0:T(8,128)} %fusion.225, f32[8,1024]{1,0:T(8,128)S(1)} %dynamic-slice_bitcast_fusion.2, bf16[2,1024,8,64]{1,3,2,0:T(8,128)(2,1)} %get-tuple-element.235), kind=kOutput, calls=%fused_computation.5.clone.1 | convolution fusion | flops 2197815296 | bytes 72385536 | tf_op jit(solution)/shard_map/while/body/eval_jaxpr/hqk,qhd->khd/dot_general | solution.py:70
  1105.5 20.7 %reduce-scatter.4.cloned.1.call-done = bf16[2,1024,512]{2,1,0:T(8,128)(2,1)} async-done(((bf16[2,2048,512]{2,1,0:T(8,128)(2,1)}), bf16[2,1024,512]{2,1,0:T(8,128)(2,1)}) %reduce-scatter.4.cloned.1.call-update) | async-done | bytes 2097168 | tf_op jit(solution)/shard_map/reduce_scatter | solution.py:254
  1212.5 89.2 %all-reduce.11.cloned.1.call-done = (bf16[2,1024,1024]{2,1,0:T(8,128)(2,1)}, bf16[2,1024,16]{1,2,0:T(8,128)(2,1)}, bf16[2,1024,16]{1,2,0:T(8,128)(2,1)}) async-done(((bf16[2,1024,1024]{2,1,0:T(8,128)(2,1)}, bf16[2,1024,16]{1,2,0:T(8,128)(2,1)}, bf16[2,1024,16]{1,2,0:T(8,128)(2,1)}), (bf16[2,1024,1024]{2,1,0:T(8,128)(2,1)}, bf16[2,1024,16]{1,2,0:T(8,128)(2,1)}, ...) | async-done | bytes 4325392 | tf_op jit(solution)/shard_map/psum | solution.py:177
  1333.0 103.8 %all-reduce.9.cloned.1.call-done = (f32[8,1024,16]{1,0,2:T(8,128)}, f32[8,16,3,512]{3,0,2,1:T(8,128)}, f32[8,512,16]{1,0,2:T(8,128)}, f32[8,16,1024]{2,0,1:T(8,1...) async-done(((f32[8,1024,16]{1,0,2:T(8,128)}, f32[8,16,3,512]{3,0,2,1:T(8,128)}, ...) | async-done | bytes 5242896 | tf_op jit(solution)/shard_map/psum | solution.py:311
  1453.4 39.8 %reduce-scatter.8.cloned.1.call-done = bf16[2,512,1024]{2,1,0:T(8,128)(2,1)} async-done(((bf16[2,1024,1024]{2,1,0:T(8,128)(2,1)}), bf16[2,512,1024]{2,1,0:T(8,128)(2,1)}) %reduce-scatter.8.cloned.1.call-update) | async-done | bytes 2097168 | tf_op jit(solution)/shard_map/reduce_scatter | solution.py:283
  (312 shorter events, 435.4 us)
Async XLA Ops:
  7.2 306.8 %copy-start = (bf16[8,16,2048]{2,1,0:T(8,128)(2,1)S(1)}, bf16[8,16,2048]{2,1,0:T(8,128)(2,1)}, u32[]{:S(2)}) copy-start(bf16[8,16,2048]{2,1,0:T(8,128)(2,1)} %param.47) | copy-start | bytes 1572868
  7.3 44.9 %all-gather.7.cloned.1.call-start = ((), (), s32[]{:S(2)}) async-start(), calls=%async_computation.3 | async-start | bytes 3538944 | tf_op jit(solution)/shard_map/all_gather | solution.py:100
  9.3 158.0 %all-gather.11.cloned.1.call-start = ((), (), s32[]{:S(2)}) async-start(), calls=%async_computation.5 | async-start | bytes 6291456 | tf_op jit(solution)/shard_map/all_gather | solution.py:137
  12.4 93.7 %copy-start.21 = (f32[2,1024,64]{1,2,0:T(8,128)}, f32[2,1024,64]{1,2,0:T(8,128)S(1)}, u32[]{:S(2)}) copy-start(f32[2,1024,64]{1,2,0:T(8,128)S(1)} %concatenate.20) | copy-start | bytes 1572868
  112.2 102.8 %copy-start.3 = (bf16[2,1024,8,64]{1,3,2,0:T(8,128)(2,1)}, bf16[2,1024,8,64]{1,3,2,0:T(8,128)(2,1)S(1)}, u32[]{:S(2)}) copy-start(bf16[2,1024,8,64]{1,3,2,0:T(8,128)(2,1)S(1)} %get-tuple-element.213) | copy-start | bytes 6291460
  112.2 144.5 %all-gather.9.cloned.1.call-start = ((), (), s32[]{:S(2)}) async-start(), calls=%async_computation.4 | async-start | bytes 6291456 | tf_op jit(solution)/shard_map/all_gather | solution.py:138
  116.9 186.6 %all-gather.13.cloned.1.call-start = ((), (), s32[]{:S(2)}) async-start(), calls=%async_computation.6 | async-start | bytes 1179648 | tf_op jit(solution)/shard_map/all_gather | solution.py:101
  117.5 201.1 %all-gather.17.cloned.1.call-start = ((), (), s32[]{:S(2)}) async-start(), calls=%async_computation.8 | async-start | bytes 4718592 | tf_op jit(solution)/shard_map/all_gather | solution.py:103
  118.0 301.0 %all-reduce.15.cloned.1.call-start = ((), (), s32[]{:S(2)}) async-start(), calls=%async_computation.15 | async-start | bytes 8519680 | tf_op jit(solution)/shard_map/psum | solution.py:152
  309.2 158.7 %all-gather.15.cloned.1.call-start = ((), (), s32[]{:S(2)}) async-start(), calls=%async_computation.7 | async-start | bytes 4718592 | tf_op jit(solution)/shard_map/all_gather | solution.py:102
  310.0 374.1 %all-reduce.13.cloned.1.call-start = ((), (), s32[]{:S(2)}) async-start(), calls=%async_computation.14 | async-start | bytes 8519680 | tf_op jit(solution)/shard_map/psum | solution.py:206
  315.0 226.7 %copy-start.40 = (bf16[2,2048,16]{1,0,2:T(2,128)(2,1)}, bf16[2,2048,16]{1,0,2:T(2,128)(2,1)S(1)}, u32[]{:S(2)}) copy-start(bf16[2,2048,16]{1,0,2:T(2,128)(2,1)S(1)} %convolution_convert_fusion.1) | copy-start | bytes 393220
  318.5 223.1 %copy-start.28 = (bf16[2,16,1024]{2,1,0:T(8,128)(2,1)}, bf16[2,16,1024]{2,1,0:T(8,128)(2,1)S(1)}, u32[]{:S(2)}) copy-start(bf16[2,16,1024]{2,1,0:T(8,128)(2,1)S(1)} %convolution_convert_fusion.7) | copy-start | bytes 196612
  318.5 100.6 %copy-start.61 = (f32[1024]{0:T(1024)S(1)}, f32[1024]{0:T(1024)}, u32[]{:S(2)}) copy-start(f32[1024]{0:T(1024)} %param.35) | copy-start | bytes 12292
  575.5 550.7 %reduce-scatter.4.cloned.1.call-start = ((), (), s32[]{:S(2)}) async-start(), calls=%async_computation.9 | async-start | bytes 6291456 | tf_op jit(solution)/shard_map/reduce_scatter | solution.py:254
  1071.7 113.9 %reduce-scatter.6.cloned.1.call-start = ((), (), s32[]{:S(2)}) async-start(), calls=%async_computation.10 | async-start | bytes 6291456 | tf_op jit(solution)/shard_map/reduce_scatter | solution.py:260
  1078.1 223.6 %all-reduce.11.cloned.1.call-start = ((), (), s32[]{:S(2)}) async-start(), calls=%async_computation.13 | async-start | bytes 8650752 | tf_op jit(solution)/shard_map/psum | solution.py:177
  1190.2 246.6 %all-reduce.9.cloned.1.call-start = ((), (), s32[]{:S(2)}) async-start(), calls=%async_computation.12 | async-start | bytes 10485760 | tf_op jit(solution)/shard_map/psum | solution.py:311
  1208.2 93.5 %copy-start.59 = (f32[2,1024]{1,0:T(2,128)S(1)}, f32[2,1024]{1,0:T(2,128)}, u32[]{:S(2)}) copy-start(f32[2,1024]{1,0:T(2,128)} %copy-done.58) | copy-start | bytes 24580
  1208.2 93.5 %copy-start.65 = (f32[1024]{0:T(1024)S(1)}, f32[1024]{0:T(1024)}, u32[]{:S(2)}) copy-start(f32[1024]{0:T(1024)} %param.30) | copy-start | bytes 12292
  1208.2 93.5 %copy-start.75 = (f32[1024]{0:T(1024)S(1)}, f32[1024]{0:T(1024)}, u32[]{:S(2)}) copy-start(f32[1024]{0:T(1024)} %param.31) | copy-start | bytes 12292
  1309.1 184.1 %reduce-scatter.8.cloned.1.call-start = ((), (), s32[]{:S(2)}) async-start(), calls=%async_computation.11 | async-start | bytes 6291456 | tf_op jit(solution)/shard_map/reduce_scatter | solution.py:283
  1333.0 160.2 %copy-start.49 = (bf16[2,1024,16]{1,0,2:T(2,128)(2,1)S(1)}, bf16[2,1024,16]{1,0,2:T(2,128)(2,1)}, u32[]{:S(2)}) copy-start(bf16[2,1024,16]{1,0,2:T(2,128)(2,1)} %copy-done.48) | copy-start | bytes 196612
  1333.0 160.2 %copy-start.62 = (bf16[2,1024,16]{1,2,0:T(8,128)(2,1)S(1)}, bf16[2,1024,16]{1,2,0:T(8,128)(2,1)}, u32[]{:S(2)}) copy-start(bf16[2,1024,16]{1,2,0:T(8,128)(2,1)} %get-tuple-element.116) | copy-start | bytes 196612
  (69 other events, 874.0 us)
Sparse Core Ops, SparseCore 0:
  10.2 41.8 all-gather.6
  112.3 54.9 all-gather.10
  169.5 56.7 all-gather.8
  227.7 23.9 all-gather.12
  253.2 46.4 all-gather.16
  309.3 109.7 all-reduce.14
  420.7 47.1 all-gather.14
  575.7 108.3 all-reduce.12
  1071.8 54.3 reduce-scatter.3
  1128.4 54.3 reduce-scatter.5
  1190.3 111.3 all-reduce.10
  1309.2 127.4 all-reduce.8
  1439.1 54.1 reduce-scatter.7
where the time goes:
time: 1520 us; the launch traced here: 1510 us
  matrix products  563 us (37%)
  waiting for transfers between devices  549 us (36%)
  other arithmetic  238 us (16%)
  local copies, waits for them, and re-layouts  143 us (9%)
    dot_general x44, matrix products, matrix_product(): return jnp.einsum(form, left, right, preferred_element_type=jnp.float32)  545 us
    psum x1, waiting for transfers between devices, shards(): lax.psum(grad_norm_part.astype(jnp.bfloat16), 'tp').astype(jnp.float32)  108 us
    convert_element_type x2, other arithmetic, clip_back(): grad_scores = (probs * (grad_probs - middle)).astype(jnp.bfloat16)  106 us
    psum x1, waiting for transfers between devices, shards(): lax.psum((by_adapter(joined_down_term), by_adapter(joined_up_term), by_ad...  104 us
    psum x1, waiting for transfers between devices, shards(): lax.psum(mlp_part.astype(jnp.bfloat16), 'tp').astype(jnp.float32)  89.2 us
    psum x1, waiting for transfers between devices, shards(): lax.psum(out_part.astype(jnp.bfloat16), 'tp').astype(jnp.float32)  85.3 us
    all_gather x1, waiting for transfers between devices, shards(): key_part = lax.all_gather(keys, 'ctx', axis=1, tiled=True)  49 us
    reduce_sum x1, other arithmetic, shards(): run_total = jnp.sum(weights, -1)  41 us
  transfers between devices with their start and end apart: 13, of which 9 were waited for; matrix products, arithmetic and copies ran while one was open for 24% of the time, Pallas kernels for 0%

commit v1 on v0

--- a/solution.py
+++ b/solution.py
@@ -1,8 +1,11 @@
+import functools
 import math
 
 import jax
 import jax.numpy as jnp
 from jax import lax
+from jax.experimental import pallas as pl
+from jax.experimental.pallas import tpu as pltpu
 from jax.sharding import PartitionSpec as P
 
 eps_norm = 1e-06
@@ -70,7 +73,7 @@
     return jnp.einsum(form, left, right, preferred_element_type=jnp.float32)
 
 
-def shards(
+def general_shards(
     tokens,
     cotangent,
     adapter_pick,
@@ -335,9 +338,666 @@
     )
 
 
+B16 = jnp.bfloat16
+F32 = jnp.float32
+VMEM_LIMIT = 60 * 2**20
+exp_scale = score_scale * math.log2(math.e)
+
+
+def dot(left, right, left_dim=1, right_dim=0):
+    return lax.dot_general(
+        left, right, (((left_dim,), (right_dim,)), ((), ())), preferred_element_type=F32
+    )
+
+
+def params():
+    return pltpu.CompilerParams(vmem_limit_bytes=VMEM_LIMIT)
+
+
+def low_lanes():
+    return lax.broadcasted_iota(jnp.int32, (1, 128), 1) < 64
+
+
+def partner(values):
+    lane = lax.broadcasted_iota(jnp.int32, (1, 128), 1) % 64 % 20
+    return jnp.where(lane < 10, pltpu.roll(values, 118, 1), pltpu.roll(values, 10, 1))
+
+
+def row_norm(values):
+    centred = values - jnp.mean(values, -1, keepdims=True)
+    inverse = lax.rsqrt(jnp.mean(centred * centred, -1, keepdims=True) + eps_norm)
+    return centred * inverse, inverse
+
+
+def back_norm(weighted, scaled, inverse):
+    return inverse * (
+        weighted
+        - jnp.mean(weighted, -1, keepdims=True)
+        - scaled * jnp.mean(weighted * scaled, -1, keepdims=True)
+    )
+
+
+def project_body(
+    side, x_ref, gain_ref, shift_ref, w_own, w_other, bias_ref, down_ref, up_ref, cos_ref, sin_ref,
+    own_q, own_k, own_v, other_q, other_k, other_v, xn_ref, u_ref,
+):
+    scaled, _ = row_norm(x_ref[...].astype(F32))
+    xn = (scaled * gain_ref[...] + shift_ref[...]).astype(B16)
+    xn_ref[...] = xn
+    u = dot(xn, down_ref[...], 1, 1).astype(B16)
+    u_ref[...] = u
+    core = side[0]
+    for w_ref, half, outs in (
+        (w_own, core, (own_q, own_k, own_v)),
+        (w_other, 1 - core, (other_q, other_k, other_v)),
+    ):
+        for part in range(3):
+            w = w_ref[:, 0, part].reshape(-1, w_ref.shape[-1])
+            value = dot(xn, w) + bias_ref[half, part] + dot(u, up_ref[half, part])
+            if part == 2:
+                outs[2][...] = value.astype(B16)
+                continue
+            for at in range(0, value.shape[1], 128):
+                piece = value[:, at : at + 128]
+                outs[part][:, at : at + 128] = (
+                    piece * cos_ref[...] + partner(piece) * sin_ref[...]
+                ).astype(B16)
+
+
+def project(side, x, gain, shift, weight, bias, down, up, cosine, sine):
+    rows, width = x.shape
+    shards_, _, _, depth, half = weight.shape
+    block = 256
+    row = lambda columns: pl.BlockSpec((block, columns), lambda i, s: (i, 0))
+    whole = lambda shape: pl.BlockSpec(shape, lambda i, s: (0,) * len(shape))
+    w_spec = lambda pick: pl.BlockSpec(
+        (shards_, 1, 3, depth, half), lambda i, s: (0, pick(s[0]), 0, 0, 0)
+    )
+    part = jax.ShapeDtypeStruct((rows, half), B16)
+    return pl.pallas_call(
+        project_body,
+        grid_spec=pltpu.PrefetchScalarGridSpec(
+            num_scalar_prefetch=1,
+            grid=(rows // block,),
+            in_specs=[
+                row(width), whole((1, width)), whole((1, width)),
+                w_spec(lambda s: s), w_spec(lambda s: 1 - s),
+                whole(bias.shape), whole(down.shape), whole(up.shape), row(128), row(128),
+            ],
+            out_specs=[row(half)] * 6 + [row(width), row(down.shape[0])],
+        ),
+        out_shape=[part] * 6
+        + [
+            jax.ShapeDtypeStruct((rows, width), B16),
+            jax.ShapeDtypeStruct((rows, down.shape[0]), B16),
+        ],
+        compiler_params=params(),
+        cost_estimate=pl.CostEstimate(
+            flops=2 * rows * width * 6 * half, bytes_accessed=16 * 2**20, transcendentals=0
+        ),
+    )(side, x, gain, shift, weight, weight, bias, down, up, cosine, sine)
+
+
+def attend_body(q_ref, k_ref, v_ref, o_ref, inv_ref, e_ref, vm_ref):
+    rows_all, length = q_ref.shape[0], k_ref.shape[0]
+    low = low_lanes()
+
+    @pl.when(pl.program_id(1) == 0)
+    def _():
+        vm_ref[0] = jnp.where(low, v_ref[...], 1).astype(B16)
+        vm_ref[1] = jnp.where(low, 1, v_ref[...]).astype(B16)
+
+    step = min(256, rows_all)
+    for at in range(0, rows_all, step):
+        rows = pl.ds(at, step)
+        q = q_ref[rows, :]
+        sums = []
+        for head in range(2):
+            mine = low if head == 0 else ~low
+            scores = dot(jnp.where(mine, q, 0).astype(B16), k_ref[...], 1, 1)
+            top = jnp.max(scores, 1, keepdims=True)
+            weights = jnp.exp2((scores - top) * exp_scale).astype(B16)
+            e_ref[head, rows, :] = weights
+            sums.append(dot(weights, vm_ref[head]))
+        total = pltpu.roll(jnp.where(low, sums[1], sums[0]), 64, 1)
+        inverse = 1.0 / total
+        o_ref[rows, :] = (jnp.where(low, sums[0], sums[1]) * inverse).astype(B16)
+        inv_ref[rows, :] = inverse
+
+
+def attend(query, key, value):
+    length, width = query.shape
+    block = min(1024, length)
+    rows = pl.BlockSpec((block, 128), lambda p, i: (i, p))
+    full = pl.BlockSpec((length, 128), lambda p, i: (0, p))
+    return pl.pallas_call(
+        attend_body,
+        grid=(width // 128, length // block),
+        in_specs=[rows, full, full],
+        out_specs=[rows, rows, pl.BlockSpec((2, block, length), lambda p, i: (p, i, 0))],
+        out_shape=[
+            jax.ShapeDtypeStruct((length, width), B16),
+            jax.ShapeDtypeStruct((length, width), F32),
+            jax.ShapeDtypeStruct((width // 64, length, length), B16),
+        ],
+        scratch_shapes=[pltpu.VMEM((2, length, 128), B16)],
+        compiler_params=params(),
+        cost_estimate=pl.CostEstimate(
+            flops=16 * length * length * width,
+            bytes_accessed=width // 64 * length * length * 2,
+            transcendentals=width // 64 * length * length,
+        ),
+    )(query, key, value)
+
+
+def attend_back_body(
+    q_ref, k_ref, v_ref, o_ref, inv_ref, g_ref, e_ref, cos_ref, sin_ref, cos_all, sin_all,
+    gq_ref, gk_ref, gv_ref, key_sum, value_sum, vm_ref,
+):
+    rows_all, length = q_ref.shape[0], k_ref.shape[0]
+    low = low_lanes()
+    at_step = pl.program_id(1)
+
+    @pl.when(at_step == 0)
+    def _():
+        key_sum[...] = jnp.zeros_like(key_sum)
+        value_sum[...] = jnp.zeros_like(value_sum)
+        vm_ref[0] = jnp.where(low, v_ref[...], -1).astype(B16)
+        vm_ref[1] = jnp.where(low, -1, v_ref[...]).astype(B16)
+
+    step = min(256, rows_all)
+    for at in range(0, rows_all, step):
+        rows = pl.ds(at, step)
+        grad = g_ref[rows, :].astype(F32) * inv_ref[rows, :]
+        grad_low = grad.astype(B16)
+        product = pltpu.roll(grad * o_ref[rows, :].astype(F32), 64, 1).astype(B16)
+        q_turned = q_ref[rows, :].T
+        g_turned = grad_low.T
+        parts = []
+        for head in range(2):
+            mine = low if head == 0 else ~low
+            weights = e_ref[head, rows, :]
+            grad_probs = dot(jnp.where(mine, grad_low, product), vm_ref[head], 1, 1)
+            grad_scores = (weights.astype(F32) * grad_probs).astype(B16)
+            parts.append(dot(grad_scores, k_ref[...]))
+            span = pl.ds(head * 64, 64)
+            key_sum[span, :] += dot(q_turned[head * 64 : head * 64 + 64], grad_scores)
+            value_sum[span, :] += dot(g_turned[head * 64 : head * 64 + 64], weights)
+        gq = jnp.where(low, parts[0], parts[1]) * score_scale
+        gq_ref[rows, :] = (gq * cos_ref[rows, :] + partner(gq * sin_ref[rows, :])).astype(B16)
+
+    @pl.when(at_step == pl.num_programs(1) - 1)
+    def _():
+        gk = key_sum[...].T * score_scale
+        gk_ref[...] = (gk * cos_all[...] + partner(gk * sin_all[...])).astype(B16)
+        gv_ref[...] = value_sum[...].T.astype(B16)
+
+
+def attend_back(query, key, value, attended, inverse, grad, weights, cosine, sine):
+    length, width = query.shape
+    block = min(512, length)
+    rows = pl.BlockSpec((block, 128), lambda p, i: (i, p))
+    full = pl.BlockSpec((length, 128), lambda p, i: (0, p))
+    table = pl.BlockSpec((block, 128), lambda p, i: (i, 0))
+    table_all = pl.BlockSpec((length, 128), lambda p, i: (0, 0))
+    return pl.pallas_call(
+        attend_back_body,
+        grid=(width // 128, length // block),
+        in_specs=[
+            rows, full, full, rows, rows, rows,
+            pl.BlockSpec((2, block, length), lambda p, i: (p, i, 0)),
+            table, table, table_all, table_all,
+        ],
+        out_specs=[rows, full, full],
+        out_shape=[jax.ShapeDtypeStruct((length, width), B16)] * 3,
+        scratch_shapes=[
+            pltpu.VMEM((128, length), F32),
+            pltpu.VMEM((128, length), F32),
+            pltpu.VMEM((2, length, 128), B16),
+        ],
+        compiler_params=params(),
+        cost_estimate=pl.CostEstimate(
+            flops=20 * length * length * width,
+            bytes_accessed=width // 64 * length * length * 2,
+            transcendentals=0,
+        ),
+    )(query, key, value, attended, inverse, grad, weights, cosine, sine, cosine, sine)
+
+
+def gauss_parts(z):
+    t = 1.0 / (1.0 + (0.3275911 * math.sqrt(0.5)) * jnp.abs(z))
+    poly = t * (0.254829592 + t * (-0.284496736 + t * (1.421413741 + t * (-1.453152027 + t * 1.061405429))))
+    bell = jnp.exp2((z * z) * (-0.5 * math.log2(math.e)))
+    upper = 0.5 * poly * bell
+    cdf = jnp.where(z >= 0, 1.0 - upper, upper)
+    return cdf, bell * (1.0 / math.sqrt(2.0 * math.pi))
+
+
+def middle_body(
+    side, x_ref, cot_ref, own_ref, other_ref, wo_ref, e_ref, r_ref,
+    out_off, gain_ref, shift_ref, wide_off, shrink_off,
+    od_ref, ou_ref, ed_ref, ru_ref, eu_ref, rd_ref,
+    output_ref, gh_ref, gown_ref, gother_ref,
+    t_od, t_ou, t_ed, t_ru, t_eu, t_rd,
+    hidden, xn_ref, total, back, u2_ref, u3_ref, u4_sum, g4_ref, g3_sum,
+):
+    f = pl.program_id(0)
+    last = pl.num_programs(0) - 1
+    core = side[0]
+    rows_all = x_ref.shape[0]
+    step = 256
+
+    def wo_half(half):
+        w = wo_ref[:, half]
+        return jnp.concatenate([w[i] for i in range(w.shape[0])], axis=1)
+
+    @pl.when(f == 0)
+    def _():
+        w_own, w_other = wo_half(core), wo_half(1 - core)
+        for at in range(0, rows_all, step):
+            rows = pl.ds(at, step)
+            own, other = own_ref[rows, :], other_ref[rows, :]
+            u2 = (dot(own, od_ref[core], 1, 1) + dot(other, od_ref[1 - core], 1, 1)).astype(B16)
+            u2_ref[rows, :] = u2
+            h = (
+                x_ref[rows, :].astype(F32) + dot(own, w_own) + dot(other, w_other)
+                + out_off[...] + dot(u2, ou_ref[...])
+            )
+            hidden[rows, :] = h
+            scaled, _ = row_norm(h)
+            xn = (scaled * gain_ref[...] + shift_ref[...]).astype(B16)
+            xn_ref[rows, :] = xn
+            u3_ref[rows, :] = dot(xn, ed_ref[...], 1, 1).astype(B16)
+            g4_ref[rows, :] = dot(cot_ref[rows, :], ru_ref[...], 1, 1).astype(B16)
+            total[rows, :] = h + shrink_off[...]
+            back[rows, :] = jnp.zeros_like(h)
+            u4_sum[rows, :] = jnp.zeros((step, u4_sum.shape[1]), F32)
+            g3_sum[rows, :] = jnp.zeros((step, g3_sum.shape[1]), F32)
+
+    w_e = e_ref[:, 0].reshape(-1, e_ref.shape[-1])
+    w_r = jnp.concatenate([r_ref[i, 0] for i in range(r_ref.shape[0])], axis=1)
+    eu, rd = eu_ref[0], rd_ref[0]
+    sum_eu, sum_rd = 0.0, 0.0
+    for at in range(0, rows_all, step):
+        rows = pl.ds(at, step)
+        u3, g4 = u3_ref[rows, :], g4_ref[rows, :]
+        z = dot(xn_ref[rows, :], w_e) + wide_off[...] + dot(u3, eu)
+        gact = dot(cot_ref[rows, :], w_r, 1, 1) + dot(g4, rd)
+        cdf, density = gauss_parts(z)
+        act = (z * cdf).astype(B16)
+        gz = (gact * (cdf + z * density)).astype(B16)
+        total[rows, :] += dot(act, w_r)
+        u4_sum[rows, :] += dot(act, rd, 1, 1)
+        back[rows, :] += dot(gz, w_e, 1, 1)
+        g3_sum[rows, :] += dot(gz, eu, 1, 1)
+        sum_rd += dot(g4, act, 0, 0)
+        sum_eu += dot(u3, gz, 0, 0)
+    t_rd[0] = sum_rd
+    t_eu[0] = sum_eu
+
+    @pl.when(f == last)
+    def _():
+        w_own, w_other = wo_half(core), wo_half(1 - core)
+        s_ru, s_ed, s_ou, s_own, s_other = 0.0, 0.0, 0.0, 0.0, 0.0
+        for at in range(0, rows_all, step):
+            rows = pl.ds(at, step)
+            cot = cot_ref[rows, :]
+            u4 = u4_sum[rows, :].astype(B16)
+            output_ref[rows, :] = (total[rows, :] + dot(u4, ru_ref[...])).astype(B16)
+            s_ru += dot(u4, cot, 0, 0)
+            g3 = g3_sum[rows, :].astype(B16)
+            s_ed += dot(g3, xn_ref[rows, :], 0, 0)
+            gx = back[rows, :] + dot(g3, ed_ref[...])
+            scaled, inverse = row_norm(hidden[rows, :])
+            gh = cot.astype(F32) + back_norm(gx * gain_ref[...], scaled, inverse)
+            gh_ref[rows, :] = gh
+            gb = gh.astype(B16)
+            s_ou += dot(u2_ref[rows, :], gb, 0, 0)
+            g2 = dot(gb, ou_ref[...], 1, 1).astype(B16)
+            s_own += dot(g2, own_ref[rows, :], 0, 0)
+            s_other += dot(g2, other_ref[rows, :], 0, 0)
+            gown_ref[rows, :] = (dot(gb, w_own, 1, 1) + dot(g2, od_ref[core])).astype(B16)
+            gother_ref[rows, :] = (dot(gb, w_other, 1, 1) + dot(g2, od_ref[1 - core])).astype(B16)
+        t_ru[...] = s_ru
+        t_ed[...] = s_ed
+        t_ou[...] = s_ou
+        t_od[core] = s_own
+        t_od[1 - core] = s_other
+
+
+def middle(
+    side, x, cot, own, other, w_o, w_e, w_r, out_off, gain, shift, wide_off, shrink_off,
+    od, ou, ed, ru, eu, rd,
+):
+    rows, width = x.shape
+    half = own.shape[1]
+    shards_, _, depth, hidden_half = w_e.shape
+    rank = ou.shape[0]
+    block = 512
+    per = hidden_half // block
+    steps = 2 * per
+    one = lambda shape: pl.BlockSpec(
+        shape, lambda f, s: (0,) * len(shape), pipeline_mode=pl.Buffered(1)
+    )
+    small = pl.BlockSpec((1, rank, block), lambda f, s: (f // per, 0, f % per))
+    full_t = jax.ShapeDtypeStruct((rank, width), F32)
+    split_t = jax.ShapeDtypeStruct((2, rank, hidden_half), F32)
+    return pl.pallas_call(
+        middle_body,
+        grid_spec=pltpu.PrefetchScalarGridSpec(
+            num_scalar_prefetch=1,
+            grid=(steps,),
+            in_specs=[
+                one((rows, width)), one((rows, width)), one((rows, half)), one((rows, half)),
+                one(w_o.shape),
+                pl.BlockSpec((shards_, 1, depth, block), lambda f, s: (0, f // per, 0, f % per)),
+                pl.BlockSpec((shards_, 1, block, w_r.shape[3]), lambda f, s: (0, f // per, f % per, 0)),
+                one((1, width)), one((1, width)), one((1, width)),
+                pl.BlockSpec((1, block), lambda f, s: (0, f)),
+                one((1, width)),
+                one(od.shape), one(ou.shape), one(ed.shape), one(ru.shape), small, small,
+            ],
+            out_specs=[
+                one((rows, width)), one((rows, width)), one((rows, half)), one((rows, half)),
+                one((2, rank, half)), one((rank, width)), one((rank, width)), one((rank, width)),
+                small, small,
+            ],
+            scratch_shapes=[
+                pltpu.VMEM((rows, width), F32), pltpu.VMEM((rows, width), B16),
+                pltpu.VMEM((rows, width), F32), pltpu.VMEM((rows, width), F32),
+                pltpu.VMEM((rows, rank), B16), pltpu.VMEM((rows, rank), B16),
+                pltpu.VMEM((rows, rank), F32), pltpu.VMEM((rows, rank), B16),
+                pltpu.VMEM((rows, rank), F32),
+            ],
+        ),
+        out_shape=[
+            jax.ShapeDtypeStruct((rows, width), B16),
+            jax.ShapeDtypeStruct((rows, width), F32),
+            jax.ShapeDtypeStruct((rows, half), B16),
+            jax.ShapeDtypeStruct((rows, half), B16),
+            jax.ShapeDtypeStruct((2, rank, half), F32),
+            full_t, full_t, full_t, split_t, split_t,
+        ],
+        compiler_params=params(),
+        cost_estimate=pl.CostEstimate(
+            flops=2 * rows * width * (16 * hidden_half // 2 + 4 * half),
+            bytes_accessed=40 * 2**20,
+            transcendentals=rows * hidden_half * 2,
+        ),
+    )(
+        side, x, cot, own, other, w_o, w_e, w_r, out_off, gain, shift, wide_off, shrink_off,
+        od, ou, ed, ru, eu, rd,
+    )
+
+
+def unproject_body(
+    side, x_ref, gh_ref, xn_ref, u_ref, gain_ref, w_own, w_other, down_ref, up_ref,
+    own_q, own_k, own_v, other_q, other_k, other_v,
+    grad_ref, t_fd, t_fu,
+):
+    core = side[0]
+    first = pl.program_id(0) == 0
+
+    @pl.when(first)
+    def _():
+        t_fd[...] = jnp.zeros_like(t_fd)
+        t_fu[...] = jnp.zeros_like(t_fu)
+
+    u = u_ref[...]
+    g1, gx = 0.0, 0.0
+    for w_ref, half, grads in (
+        (w_own, core, (own_q, own_k, own_v)),
+        (w_other, 1 - core, (other_q, other_k, other_v)),
+    ):
+        for part in range(3):
+            grad = grads[part][...]
+            w = w_ref[:, 0, part].reshape(-1, w_ref.shape[-1])
+            gx += dot(grad, w, 1, 1)
+            g1 += dot(grad, up_ref[half, part], 1, 1)
+            t_fu[half, part] += dot(u, grad, 0, 0)
+    g1 = g1.astype(B16)
+    t_fd[...] += dot(g1, xn_ref[...], 0, 0)
+    gx += dot(g1, down_ref[...])
+    scaled, inverse = row_norm(x_ref[...].astype(F32))
+    grad_ref[...] = (gh_ref[...] + back_norm(gx * gain_ref[...], scaled, inverse)).astype(B16)
+
+
+def unproject(side, x, gh, xn, u, gain, weight, down, up, own, other):
+    rows, width = x.shape
+    shards_, _, _, depth, half = weight.shape
+    rank = down.shape[0]
+    block = 256
+    row = lambda columns: pl.BlockSpec((block, columns), lambda i, s: (i, 0))
+    whole = lambda shape: pl.BlockSpec(shape, lambda i, s: (0,) * len(shape))
+    w_spec = lambda pick: pl.BlockSpec(
+        (shards_, 1, 3, depth, half), lambda i, s: (0, pick(s[0]), 0, 0, 0)
+    )
+    return pl.pallas_call(
+        unproject_body,
+        grid_spec=pltpu.PrefetchScalarGridSpec(
+            num_scalar_prefetch=1,
+            grid=(rows // block,),
+            in_specs=[
+                row(width), row(width), row(width), row(rank), whole((1, width)),
+                w_spec(lambda s: s), w_spec(lambda s: 1 - s), whole(down.shape), whole(up.shape),
+            ]
+            + [row(half)] * 6,
+            out_specs=[row(width), whole((rank, width)), whole(up.shape)],
+        ),
+        out_shape=[
+            jax.ShapeDtypeStruct((rows, width), B16),
+            jax.ShapeDtypeStruct((rank, width), F32),
+            jax.ShapeDtypeStruct(up.shape, F32),
+        ],
+        compiler_params=params(),
+        cost_estimate=pl.CostEstimate(
+            flops=2 * rows * width * 6 * half, bytes_accessed=20 * 2**20, transcendentals=0
+        ),
+    )(side, x, gh, xn, u, gain, weight, weight, down, up, *own, *other)
+
+
+def clip_shards(
+    planes,
+    tokens,
+    cotangent,
+    adapter_pick,
+    positions,
+    first_gain,
+    first_shift,
+    joined_weight,
+    joined_bias,
+    output_weight,
+    mixing_exit_offset,
+    second_gain,
+    second_shift,
+    expand_weight,
+    widening_offset,
+    reduce_weight,
+    shrinking_offset,
+    joined_down,
+    joined_up,
+    output_down,
+    output_up,
+    expand_down,
+    expand_up,
+    reduce_down,
+    reduce_up,
+):
+    core = lax.axis_index("shard") % 2
+    ctx = lax.axis_index("ctx")
+    tp = lax.axis_index("tp")
+    side = jnp.reshape(core, (1,)).astype(jnp.int32)
+    cores = [(i, i ^ 1) for i in range(2 * planes)]
+    pair = [(0, 1), (1, 0)]
+    place = lambda z, c, x: (2 * z + c) * 2 + x
+    turns = [
+        (place(z, c, x), place(z, x, c)) for z in range(planes) for c in range(2) for x in range(2)
+    ]
+    turns_flip = [(2 * a + y, 2 * b + 1 - y) for a, b in turns for y in range(2)]
+
+    def turn(array):
+        return lax.ppermute(array, ("shard", "ctx"), turns)
+
+    def to_core(array):
+        return lax.ppermute(array, "shard", cores)
+
+    def to_tp(array):
+        return lax.ppermute(array, "tp", pair)
+
+    def to_ctx(array):
+        return lax.ppermute(array, "ctx", pair)
+
+    def by_tp(mine, others):
+        return jnp.where(tp == 0, jnp.stack([mine, others]), jnp.stack([others, mine]))
+
+    mine_of = lambda array, axis=0: lax.dynamic_index_in_dim(array, tp, axis, keepdims=False)
+
+    def gather(weight):
+        whole = lax.all_gather(weight, ("shard", "tp"), axis=0, tiled=False)
+        return whole.reshape((2 * planes, 2) + weight.shape)
+
+    x = turn(mine_of(tokens))
+    w_j = gather(jnp.transpose(joined_weight, (1, 0, 2)))
+    places = turn(mine_of(positions, 1))
+    cot = turn(mine_of(cotangent))
+    w_o = gather(output_weight)
+    w_e = gather(expand_weight)
+    w_r = gather(reduce_weight)
+
+    away = to_core(adapter_pick)
+    picks = jnp.where(core == ctx, adapter_pick, away)
+    pick = lax.dynamic_index_in_dim(picks, tp, 0, keepdims=False)
+    pick_next = lax.dynamic_index_in_dim(picks, 1 - tp, 0, keepdims=False)
+
+    def row(table, at):
+        return lax.dynamic_index_in_dim(table, at, 0, keepdims=False)
+
+    def split_factors(at):
+        ju, od, eu, rd = row(joined_up, at), row(output_down, at), row(expand_up, at), row(reduce_down, at)
+        return jnp.concatenate([ju.reshape(ju.shape[0], -1), od.T, eu, rd.T], axis=1)
+
+    packed = by_tp(split_factors(pick), to_tp(split_factors(pick_next)))
+    half = joined_weight.shape[2]
+    hidden_half = expand_weight.shape[1]
+    rank = joined_up.shape[1]
+    ju = jnp.transpose(packed[:, :, : 3 * half].reshape(2, rank, 3, half), (0, 2, 1, 3))
+    od = packed[:, :, 3 * half : 4 * half]
+    eu = packed[:, :, 4 * half : 4 * half + hidden_half]
+    rd = packed[:, :, 4 * half + hidden_half :]
+    jd, ed = row(joined_down, pick).T, row(expand_down, pick).T
+    ou, ru = row(output_up, pick), row(reduce_up, pick)
+    offsets = jnp.concatenate([joined_bias.reshape(-1), widening_offset])[None]
+    offsets = by_tp(offsets, to_tp(offsets))
+    bias = offsets[:, :, : 3 * half].reshape(2, 3, 1, half)
+    wide_off = offsets[:, 0, 3 * half :].reshape(1, 2 * hidden_half)
+
+    places_all = jnp.concatenate([places, to_core(places)], axis=1).astype(F32)
+    lane = jnp.arange(128, dtype=jnp.int32) % 64
+    within = lane % 20
+    rates = jnp.exp((within % 10).astype(F32) * (-math.log(10000.0) / 10.0))
+    spot = jnp.where(
+        lane < 20, places_all[0][:, None], jnp.where(lane < 40, places_all[1][:, None], places_all[2][:, None])
+    )
+    angle = spot * rates
+    turned = lane < 60
+    cosine = jnp.where(turned, jnp.cos(angle), 1.0)
+    sine = jnp.where(turned, jnp.where(within < 10, -jnp.sin(angle), jnp.sin(angle)), 0.0)
+    rows = x.shape[0]
+
+    *qkv, xn1, u1 = project(
+        side, x, first_gain[None], first_shift[None], w_j, bias, jd, ju, cosine[:rows], sine[:rows]
+    )
+    query, key, value = (
+        jnp.concatenate([mine, to_core(sent)], axis=0) for mine, sent in zip(qkv[:3], qkv[3:])
+    )
+    attended, inverse, weights = attend(query, key, value)
+    own_heads, other_heads = attended[:rows], to_core(attended[rows:])
+    out, gh, gown, gother, t_od, t_ou, t_ed, t_ru, t_eu, t_rd = middle(
+        side, x, cot, own_heads, other_heads, w_o, w_e, w_r,
+        mixing_exit_offset[None], second_gain[None], second_shift[None], wide_off, shrinking_offset[None],
+        od, ou, ed, ru, eu, rd,
+    )
+    out = turn(out)
+    output = by_tp(out, to_tp(out))
+    grad_att = jnp.concatenate([gown, to_core(gother)], axis=0)
+    grads = attend_back(query, key, value, attended, inverse, grad_att, weights, cosine, sine)
+    tokens_part, t_fd, t_fu = unproject(
+        side, x, gh, xn1, u1, first_gain[None], w_j, jd, ju,
+        [g[:rows] for g in grads], [to_core(g[rows:]) for g in grads],
+    )
+    quarter = rows // 2
+    stay = lax.dynamic_slice_in_dim(tokens_part, tp * quarter, quarter, 0)
+    leave = lax.dynamic_slice_in_dim(tokens_part, (1 - tp) * quarter, quarter, 0)
+    tokens_grad = by_tp(turn(stay), lax.ppermute(leave, ("shard", "ctx", "tp"), turns_flip))
+
+    def spread(split, full):
+        low_rank = rank // 2
+        split_parts = jnp.concatenate(split, axis=2)
+        full_part = jnp.concatenate(full, axis=1)
+        wide = jnp.concatenate([split_parts[0], split_parts[1], full_part], axis=1)
+        keep = lax.dynamic_slice_in_dim(wide, core * low_rank, low_rank, 0)
+        send = lax.dynamic_slice_in_dim(wide, (1 - core) * low_rank, low_rank, 0)
+        total = (keep + to_core(send.astype(B16)).astype(F32)).astype(B16)
+        width = split_parts.shape[2]
+        tag = jnp.full((low_rank, 128), pick.astype(B16))
+        rest = jnp.concatenate([total[:, 2 * width :], tag], axis=1)
+        keep = jnp.concatenate([lax.dynamic_slice_in_dim(total, tp * width, width, 1), rest], axis=1)
+        send = jnp.concatenate([lax.dynamic_slice_in_dim(total, (1 - tp) * width, width, 1), rest], axis=1)
+        stack = jnp.stack([keep, to_tp(send)])
+        stack = jnp.concatenate([stack, to_ctx(stack)], axis=0)
+        stacks = [stack]
+        for shift in range(1, planes):
+            stacks.append(
+                lax.ppermute(stack, "shard", [(i, (i + 2 * shift) % (2 * planes)) for i in range(2 * planes)])
+            )
+        stack = jnp.concatenate(stacks, axis=0)
+        others = to_core(stack)
+        stack = jnp.where(
+            core == 0,
+            jnp.concatenate([stack, others], axis=1),
+            jnp.concatenate([others, stack], axis=1),
+        )
+        chosen = stack[:, 0, -1].astype(F32)
+        choose = (chosen[None, :] == jnp.arange(joined_down.shape[0], dtype=F32)[:, None]).astype(B16)
+        summed = lax.dot_general(
+            choose, stack[:, :, :-128], (((1,), (0,)), ((), ())), preferred_element_type=F32
+        )
+        pieces = []
+        at = 0
+        for item in split:
+            pieces.append(summed[:, :, at : at + item.shape[2]])
+            at += item.shape[2]
+        for item in full:
+            pieces.append(summed[:, :, at : at + item.shape[1]])
+            at += item.shape[1]
+        return pieces
+
+    s_od, s_eu, s_rd, s_ou, s_ed, s_ru = spread([t_od, t_eu, t_rd], [t_ou, t_ed, t_ru])
+    t_fu = jnp.transpose(t_fu, (0, 2, 1, 3)).reshape(2, rank, 3 * half)
+    s_fu, s_fd = spread([t_fu], [t_fd])
+    turn_last = lambda array: jnp.swapaxes(array, 1, 2)
+    return (
+        output,
+        tokens_grad,
+        turn_last(s_fd),
+        s_fu.reshape(s_fu.shape[0], rank, 3, half),
+        turn_last(s_od),
+        s_ou,
+        turn_last(s_ed),
+        s_eu,
+        turn_last(s_rd),
+        s_ru,
+    )
+
+
 def solution(mesh):
+    sizes = dict(mesh.shape)
+    if sizes["ctx"] == 2 and sizes["tp"] == 2 and sizes["shard"] % 2 == 0:
+        body = functools.partial(clip_shards, sizes["shard"] // 2)
+    else:
+        body = general_shards
     return jax.shard_map(
-        shards,
+        body,
         mesh=mesh,
         in_specs=(
             P("shard", "ctx", None),

time: 1520 us -> 611 us (0.40)
  matrix products: 563 us -> 4.65 us
  waiting for transfers between devices: 549 us -> 179 us
  Pallas kernels: 0 us -> 243 us
  other arithmetic: 238 us -> 24.9 us
  local copies, waits for them, and re-layouts: 143 us -> 63.2 us
  starting transfers between devices: 1.38 us -> 66.4 us
    dot_general x60 -> x2, matrix products: 563 us -> 4.65 us  [spread(): lax.dot_general(choose, stack[:, :, :-128], (((1,), (0,)), ((), ())), pre...]
    psum x4 -> x0, waiting for transfers between devices: 387 us -> none  [the longest x1 108 us: shards(): lax.psum(grad_norm_part.astype(jnp.bfloat16), 'tp').astype(jnp.float32)]
    pallas_call x0 -> x5, Pallas kernels: none -> 243 us  [the longest x1 79 us: middle(): pl.pallas_call(middle_body, grid_spec=pltpu.PrefetchScalarGridSpec(num_sc...]
    convert_element_type x7 -> x4, other arithmetic: 160 us -> 0.52 us  [the longest x2 0.47 us: spread(): chosen = stack[:, 0, -1].astype(F32)]
    ppermute x0 -> x33, starting transfers between devices: none -> 66.2 us  [the longest x5 46.9 us: turn(): return lax.ppermute(array, ('shard', 'ctx'), turns)]
    reduce_scatter x3 -> x0, waiting for transfers between devices: 60.5 us -> none  [the longest x1 39.8 us: shards(): lax.psum_scatter(grad_norm_one_part.astype(jnp.bfloat16), 'tp', scatter_d...]
    ppermute x0 -> x33, waiting for transfers between devices: none -> 60.4 us  [the longest x1 35.5 us: clip_shards(): lax.ppermute(leave, ('shard', 'ctx', 'tp'), turns_flip)]
    reduce_sum x4 -> x0, other arithmetic: 48.1 us -> none  [the longest x1 41 us: shards(): run_total = jnp.sum(weights, -1)]
  transfers between devices with their start and end apart: 13 -> 37, of which waited for: 9 -> 10; matrix products, arithmetic and copies ran while one was open for 24% -> 14% of each run, Pallas kernels for 0% -> 27%
where the time goes in v1:
time: 611 us; the launch traced here: 600 us
  Pallas kernels  243 us (40%)
  waiting for transfers between devices  179 us (29%)
  starting transfers between devices  66.4 us (11%)
  local copies, waits for them, and re-layouts  63.2 us (10%)
  other arithmetic  24.9 us (4%)
  between operations  19.3 us (3%)
    all_gather x4, waiting for transfers between devices, gather(): whole = lax.all_gather(weight, ('shard', 'tp'), axis=0, tiled=False)  115 us
    pallas_call x1, Pallas kernels, middle(): pl.pallas_call(middle_body, grid_spec=pltpu.PrefetchScalarGridSpec(num_sc...  79 us
    pallas_call x1, Pallas kernels, attend_back(): pl.pallas_call(attend_back_body, grid=(width // 128, length // block), in...  74.6 us
    pallas_call x1, Pallas kernels, attend(): pl.pallas_call(attend_body, grid=(width // 128, length // block), in_spec...  56 us
    ppermute x5, starting transfers between devices, turn(): return lax.ppermute(array, ('shard', 'ctx'), turns)  46.9 us
    ppermute x1, waiting for transfers between devices, clip_shards(): lax.ppermute(leave, ('shard', 'ctx', 'tp'), turns_flip)  35.5 us
    unnamed x61, local copies, waits for them, and re-layouts  21.7 us
    pallas_call x1, Pallas kernels, unproject(): pl.pallas_call(unproject_body, grid_spec=pltpu.PrefetchScalarGridSpec(num...  18.4 us
  transfers between devices with their start and end apart: 37, of which 10 were waited for; matrix products, arithmetic and copies ran while one was open for 14% of the time, Pallas kernels for 27%

profile of v1, /device:TPU:0, one launch (start us, length us, event | category | flops | bytes accessed | tf_op | source)
XLA Modules:
  0.0 600.0 jit_solution(6752839870601377278)
XLA Ops:
  12.1 3.1 dynamic-slice_bitcast_fusion.1
  15.2 17.2 %collective-permute-start = (bf16[1024,1024]{1,0:T(8,128)(2,1)}, bf16[1024,1024]{1,0:T(8,128)(2,1)}, u32[]{:S(2)}, u32[]{:S(2)}) collective-permute-start(bf16[1024,1024]{1,0:T(8,128)(2,1)} %dynamic-slice_bitcast_fusion.1), channel_id=1, source_target_pairs={{0,0},{2,4},{4,2},{6,6},{8,8},{10,12},{12,10},{14,14},{16,16},{18,... | collective-permute-start | bytes 6291464 | tf_op jit(solution)/shard_map/ppermute | solution.py:839
  45.2 9.5 %fusion.4 = (f32[2048,128]{1,0:T(8,128)S(1)}, f32[2048,128]{1,0:T(8,128)S(1)}) fusion(f32[128]{0:T(128)S(1)} %fusion.19, f32[2048]{0:T(1024)S(1)} %bitcast.146, f32[2048]{0:T(1024)S(1)} %bitcast.145, f32[2048]{0:T(1024)S(1)} %bitcast.144, pred[128]{0:T(512)(128)(4,1)S(1)} %get-tuple-element.146, pred[128]{0:T(512)(128)(4,1)S(1)} %get-tuple-element.147, ...), kind=kLoop, calls=%fused_computation.12 | loop fusion | flops 1835008 | bytes 2122752 | tf_op jit(solution)/shard_map/jit(_where)/select_n | solution.py:904
  57.1 19.9 %all-gather.9.cloned.1.call-done = bf16[48,128,512]{2,1,0:T(8,128)(2,1)} async-done(((bf16[3,128,512]{2,1,0:T(8,128)(2,1)}), bf16[48,128,512]{2,1,0:T(8,128)(2,1)}) %all-gather.9.cloned.1.call-update) | async-done | bytes 6291472 | tf_op jit(solution)/shard_map/all_gather | solution.py:856
  77.0 15.1 %shard_map.303 = (bf16[1024,512]{1,0:T(8,128)(2,1)}, bf16[1024,512]{1,0:T(8,128)(2,1)}, bf16[1024,512]{1,0:T(8,128)(2,1)}, bf16[1024,512]{1,0:T(8,128)(2,1)}, bf...) custom-call(s32[1]{0:T(128)} %bitcast.side, ...), custom_call_target="tpu_custom_call" | custom-call | flops 6442450944 | bytes 16777216 | tf_op jit(solution)/shard_map/pallas_call | solution.py:417
  109.5 56.0 %shard_map.304 = (bf16[2048,512]{1,0:T(8,128)(2,1)}, f32[2048,512]{1,0:T(8,128)}, bf16[8,2048,2048]{2,1,0:T(8,128)(2,1)}) custom-call(bf16[2048,512]{1,0:T(8,128)(2,1)} %constant_dynamic-update-slice_fusion.1.q_ref, bf16[2048,512]{1,0:T(8,128)(2,1)} %constant_dynamic-update-slice_fusion.3.k_ref, bf16[2048,512]{1,0:T(8,128)(2,1)} %constant_dynamic-update-slice_fusion.5.v_ref), custom_call_target="tpu_custom_call" | custom-call | flops 34359738368 | bytes 67108864 | tf_op jit(solution)/shard_map/pallas_call | solution.py:473
  165.5 3.0 fusion.24
  174.8 20.4 %all-gather.13.cloned.1.call-done = bf16[2048,2048]{1,0:T(8,128)(2,1)} async-done(((bf16[128,2048]{1,0:T(8,128)(2,1)}), bf16[2048,2048]{1,0:T(8,128)(2,1)}) %all-gather.13.cloned.1.call-update) | async-done | bytes 8388624 | tf_op jit(solution)/shard_map/all_gather | solution.py:856
  195.2 75.3 %all-gather.15.cloned.1.call-done = bf16[32768,128]{1,0:T(8,128)(2,1)} async-done(((bf16[2048,128]{1,0:T(8,128)(2,1)}), bf16[32768,128]{1,0:T(8,128)(2,1)}) %all-gather.15.cloned.1.call-update) | async-done | bytes 8388624 | tf_op jit(solution)/shard_map/all_gather | solution.py:856
  270.4 79.0 %shard_map.305 = (bf16[1024,1024]{1,0:T(8,128)(2,1)}, f32[1024,1024]{1,0:T(8,128)}, bf16[1024,512]{1,0:T(8,128)(2,1)}, bf16[1024,512]{1,0:T(8,128)(2,1)}, f32[2,...) custom-call(s32[1]{0:T(128)} %bitcast.side, ...), custom_call_target="tpu_custom_call" | custom-call | flops 38654705664 | bytes 41943040 | tf_op jit(solution)/shard_map/pallas_call | solution.py:685
  353.7 17.2 %collective-permute-start.11 = (bf16[1024,1024]{1,0:T(8,128)(2,1)}, bf16[1024,1024]{1,0:T(8,128)(2,1)}, u32[]{:S(2)}, u32[]{:S(2)}) collective-permute-start(bf16[1024,1024]{1,0:T(8,128)(2,1)} %get-tuple-element.44), channel_id=1, source_target_pairs={{0,0},{2,4},{4,2},{6,6},{8,8},{10,12},{12,10},{14,14},{16,16},{18,... | collective-permute-start | bytes 6291464 | tf_op jit(solution)/shard_map/ppermute | solution.py:839
  371.7 4.3 collective-permute-done.27
  376.2 10.9 %collective-permute-done.28 = bf16[2,8,7808]{2,1,0:T(8,128)(2,1)S(1)} collective-permute-done((bf16[2,8,7808]{2,1,0:T(8,128)(2,1)S(1)}, bf16[2,8,7808]{2,1,0:T(8,128)(2,1)S(1)}, u32[]{:S(2)}, u32[]{:S(2)}) %collective-permute-start.28) | collective-permute-done | bytes 249888 | tf_op jit(solution)/shard_map/ppermute | solution.py:848
  390.8 74.6 %shard_map.306 = (bf16[2048,512]{1,0:T(8,128)(2,1)}, bf16[2048,512]{1,0:T(8,128)(2,1)}, bf16[2048,512]{1,0:T(8,128)(2,1)}) custom-call(bf16[2048,512]{1,0:T(8,128)(2,1)} %constant_dynamic-update-slice_fusion.1.q_ref, bf16[2048,512]{1,0:T(8,128)(2,1)} %constant_dynamic-update-slice_fusion.3.k_ref, ...), custom_call_target="tpu_custom_call" | custom-call | flops 42949672960 | bytes 67108864 | tf_op jit(solution)/shard_map/pallas_call | solution.py:543
  477.4 18.4 %shard_map.307 = (bf16[1024,1024]{1,0:T(8,128)(2,1)}, f32[16,1024]{1,0:T(8,128)}, f32[2,3,16,512]{3,2,1,0:T(8,128)}) custom-call(s32[1]{0:T(128)} %bitcast.side, bf16[1024,1024]{1,0:T(8,128)(2,1)} %collective-permute-done.x_ref, f32[1024,1024]{1,0:T(8,128)} %get-tuple-element.45.gh_ref, bf16[1024,1024]{1,0:T(8,128)(2,1)} %get-tuple-element.46.xn_ref, ...), custom_call_target="tpu_custom_call" | custom-call | flops 6442450944 | bytes 20971520 | tf_op jit(solution)/shard_map/pallas_call | solution.py:775
  500.4 3.4 collective-permute-done.20
  504.2 4.5 collective-permute-done.21
  513.8 3.1 constant_dynamic-slice_fusion.5
  518.2 9.5 %collective-permute-start.17 = (bf16[512,1024]{1,0:T(8,128)(2,1)}, bf16[512,1024]{1,0:T(8,128)(2,1)}, u32[]{:S(2)}, u32[]{:S(2)}) collective-permute-start(bf16[512,1024]{1,0:T(8,128)(2,1)} %get-tuple-element.109), channel_id=1, source_target_pairs={{0,0},{2,4},{4,2},{6,6},{8,8},{10,12},{12,10},{14,14},{16,16},{18,... | collective-permute-start | bytes 3145736 | tf_op jit(solution)/shard_map/ppermute | solution.py:839
  529.4 2.9 maximum_select_fusion.1
  533.0 4.3 fusion
  545.0 35.5 %collective-permute-done.18 = bf16[512,1024]{1,0:T(8,128)(2,1)} collective-permute-done((bf16[512,1024]{1,0:T(8,128)(2,1)}, bf16[512,1024]{1,0:T(8,128)(2,1)}, u32[]{:S(2)}, u32[]{:S(2)}) %collective-permute-start.18) | collective-permute-done | bytes 1048608 | tf_op jit(solution)/shard_map/ppermute | solution.py:931
  580.5 3.9 maximum_select_fusion.2
  587.7 5.5 maximum_select_fusion
  (205 shorter events, 84.4 us)
Async XLA Ops:
  7.2 69.8 %all-gather.9.cloned.1.call-start = ((), (), s32[]{:S(2)}) async-start(), calls=%async_computation | async-start | bytes 6684672 | tf_op jit(solution)/shard_map/all_gather | solution.py:856
  7.9 166.9 %all-gather.11.cloned.1.call-start = ((), (), s32[]{:S(2)}) async-start(), calls=%async_computation.1 | async-start | bytes 2228224 | tf_op jit(solution)/shard_map/all_gather | solution.py:856
  8.7 186.5 %all-gather.13.cloned.1.call-start = ((), (), s32[]{:S(2)}) async-start(), calls=%async_computation.2 | async-start | bytes 8912896 | tf_op jit(solution)/shard_map/all_gather | solution.py:856
  9.4 261.0 %all-gather.15.cloned.1.call-start = ((), (), s32[]{:S(2)}) async-start(), calls=%async_computation.3 | async-start | bytes 8912896 | tf_op jit(solution)/shard_map/all_gather | solution.py:856
  10.0 25.2 %collective-permute-start.3 = (s32[2]{0:T(128)}, s32[2]{0:T(128)S(1)}, u32[]{:S(2)}, u32[]{:S(2)}) collective-permute-start(s32[2]{0:T(128)} %param.26), channel_id=1, source_target_pairs={{0,4},{4,0},{8,12},{12,8},{16,20},{20,16},{24,28},{28,24},{1,5},{5... | collective-permute-start | bytes 32 | tf_op jit(solution)/shard_map/ppermute | solution.py:842
  11.3 32.7 %collective-permute-start.5 = (s32[3,1024]{1,0:T(4,128)S(1)}, s32[3,1024]{1,0:T(4,128)S(1)}, u32[]{:S(2)}, u32[]{:S(2)}) collective-permute-start(s32[3,1024]{1,0:T(4,128)S(1)} %bitcast.147), channel_id=1, source_target_pairs={{0,0},{2,4},{4,2},{6,6},{8,8},{10,12},{12,10},{14,14},{16,16},{18,... | collective-permute-start | bytes 36872 | tf_op jit(solution)/shard_map/ppermute | solution.py:839
  15.2 41.9 %collective-permute-start = (bf16[1024,1024]{1,0:T(8,128)(2,1)}, bf16[1024,1024]{1,0:T(8,128)(2,1)}, u32[]{:S(2)}, u32[]{:S(2)}) collective-permute-start(bf16[1024,1024]{1,0:T(8,128)(2,1)} %dynamic-slice_bitcast_fusion.1), channel_id=1, source_target_pairs={{0,0},{2,4},{4,2},{6,6},{8,8},{10,12},{12,10},{14,14},{16,16},{18,... | collective-permute-start | bytes 6291464 | tf_op jit(solution)/shard_map/ppermute | solution.py:839
  43.2 13.3 %collective-permute-start.4 = (bf16[16,6144]{1,0:T(8,128)(2,1)S(1)}, bf16[16,6144]{1,0:T(8,128)(2,1)S(1)}, u32[]{:S(2)}, u32[]{:S(2)}) collective-permute-start(bf16[16,6144]{1,0:T(8,128)(2,1)S(1)} %pad_maximum_fusion.3), channel_id=1, source_target_pairs={{0,1},{1,0},{2,3},{3,2},{4,5},{5,4},{6,7},{7,6},{8,9},{9,8},{10,11... | collective-permute-start | bytes 589832 | tf_op jit(solution)/shard_map/ppermute | solution.py:845
  92.4 12.5 %collective-permute-start.8 = (bf16[1024,512]{1,0:T(8,128)(2,1)}, bf16[1024,512]{1,0:T(8,128)(2,1)}, u32[]{:S(2)}, u32[]{:S(2)}) collective-permute-start(bf16[1024,512]{1,0:T(8,128)(2,1)} %get-tuple-element.40), channel_id=1, source_target_pairs={{0,4},{4,0},{8,12},{12,8},{16,20},{20,16},{24,28},{28,24},{1,5},{5... | collective-permute-start | bytes 3145736 | tf_op jit(solution)/shard_map/ppermute | solution.py:842
  92.7 14.5 %collective-permute-start.7 = (bf16[1024,512]{1,0:T(8,128)(2,1)}, bf16[1024,512]{1,0:T(8,128)(2,1)}, u32[]{:S(2)}, u32[]{:S(2)}) collective-permute-start(bf16[1024,512]{1,0:T(8,128)(2,1)} %get-tuple-element.38), channel_id=1, source_target_pairs={{0,4},{4,0},{8,12},{12,8},{16,20},{20,16},{24,28},{28,24},{1,5},{5... | collective-permute-start | bytes 3145736 | tf_op jit(solution)/shard_map/ppermute | solution.py:842
  94.7 80.1 %collective-permute-start.1 = (bf16[1024,1024]{1,0:T(8,128)(2,1)S(1)}, bf16[1024,1024]{1,0:T(8,128)(2,1)}, u32[]{:S(2)}, u32[]{:S(2)}) collective-permute-start(bf16[1024,1024]{1,0:T(8,128)(2,1)S(1)} %dynamic-slice_bitcast_fusion), channel_id=1, source_target_pairs={{0,0},{2,4},{4,2},{6,6},{8,8},{10,12},{12,10},{14,14},{16,16},{18,... | collective-permute-start | bytes 6291464 | tf_op jit(solution)/shard_map/ppermute | solution.py:839
  352.4 18.5 %collective-permute-start.26 = (bf16[8,12288]{1,0:T(8,128)(2,1)S(1)}, bf16[8,12288]{1,0:T(8,128)(2,1)S(1)}, u32[]{:S(2)}, u32[]{:S(2)}) collective-permute-start(bf16[8,12288]{1,0:T(8,128)(2,1)S(1)} %dynamic-slice_convert_fusion), channel_id=1, source_target_pairs={{0,4},{4,0},{8,12},{12,8},{16,20},{20,16},{24,28},{28,24},{1,5},{5... | collective-permute-start | bytes 589832 | tf_op jit(solution)/shard_map/ppermute | solution.py:842
  353.4 35.9 %collective-permute-start.13 = (bf16[1024,512]{1,0:T(8,128)(2,1)}, bf16[1024,512]{1,0:T(8,128)(2,1)S(1)}, u32[]{:S(2)}, u32[]{:S(2)}) collective-permute-start(bf16[1024,512]{1,0:T(8,128)(2,1)} %get-tuple-element.50), channel_id=1, source_target_pairs={{0,4},{4,0},{8,12},{12,8},{16,20},{20,16},{24,28},{28,24},{1,5},{5... | collective-permute-start | bytes 3145736 | tf_op jit(solution)/shard_map/ppermute | solution.py:842
  353.7 159.5 %collective-permute-start.11 = (bf16[1024,1024]{1,0:T(8,128)(2,1)}, bf16[1024,1024]{1,0:T(8,128)(2,1)}, u32[]{:S(2)}, u32[]{:S(2)}) collective-permute-start(bf16[1024,1024]{1,0:T(8,128)(2,1)} %get-tuple-element.44), channel_id=1, source_target_pairs={{0,0},{2,4},{4,2},{6,6},{8,8},{10,12},{12,10},{14,14},{16,16},{18,... | collective-permute-start | bytes 6291464 | tf_op jit(solution)/shard_map/ppermute | solution.py:839
  387.1 84.2 %collective-permute-start.29 = (bf16[4,8,7808]{2,1,0:T(8,128)(2,1)S(1)}, bf16[4,8,7808]{2,1,0:T(8,128)(2,1)}, u32[]{:S(2)}, u32[]{:S(2)}) collective-permute-start(bf16[4,8,7808]{2,1,0:T(8,128)(2,1)S(1)} %pad_maximum_fusion.1), channel_id=1, source_target_pairs={{0,8},{4,12},{8,16},{12,20},{16,24},{20,28},{24,0},{28,4},{1,9},{5... | collective-permute-start | bytes 1499144 | tf_op jit(solution)/shard_map/ppermute | solution.py:951
  388.1 84.8 %collective-permute-start.30 = (bf16[4,8,7808]{2,1,0:T(8,128)(2,1)S(1)}, bf16[4,8,7808]{2,1,0:T(8,128)(2,1)}, u32[]{:S(2)}, u32[]{:S(2)}) collective-permute-start(bf16[4,8,7808]{2,1,0:T(8,128)(2,1)S(1)} %pad_maximum_fusion.1), channel_id=1, source_target_pairs={{0,16},{4,20},{8,24},{12,28},{16,0},{20,4},{24,8},{28,12},{1,17},{... | collective-permute-start | bytes 1499144 | tf_op jit(solution)/shard_map/ppermute | solution.py:951
  472.9 25.1 %collective-permute-start.31 = (bf16[4,8,7808]{2,1,0:T(8,128)(2,1)S(1)}, bf16[4,8,7808]{2,1,0:T(8,128)(2,1)}, u32[]{:S(2)}, u32[]{:S(2)}) collective-permute-start(bf16[4,8,7808]{2,1,0:T(8,128)(2,1)S(1)} %pad_maximum_fusion.1), channel_id=1, source_target_pairs={{0,24},{4,28},{8,0},{12,4},{16,8},{20,12},{24,16},{28,20},{1,25},{... | collective-permute-start | bytes 1499144 | tf_op jit(solution)/shard_map/ppermute | solution.py:951
  499.1 30.3 %collective-permute-start.32 = (bf16[16,8,7808]{2,1,0:T(8,128)(2,1)S(1)}, bf16[16,8,7808]{2,1,0:T(8,128)(2,1)}, u32[]{:S(2)}, u32[]{:S(2)}) collective-permute-start(bf16[16,8,7808]{2,1,0:T(8,128)(2,1)S(1)} %constant_dynamic-update-slice_fusion.16), channel_id=1, source_target_pairs={{0,4},{4,0},{8,12},{12,8},{16,20},{20,16},{24,28},{28,24},{1,5},{5... | collective-permute-start | bytes 5996552 | tf_op jit(solution)/shard_map/ppermute | solution.py:842
  509.0 18.7 %collective-permute-start.23 = (bf16[4,8,2688]{2,0,1:T(4,128)(2,1)S(1)}, bf16[4,8,2688]{2,0,1:T(4,128)(2,1)S(1)}, u32[]{:S(2)}, u32[]{:S(2)}) collective-permute-start(bf16[4,8,2688]{2,0,1:T(4,128)(2,1)S(1)} %pad_maximum_fusion.6), channel_id=1, source_target_pairs={{0,16},{4,20},{8,24},{12,28},{16,0},{20,4},{24,8},{28,12},{1,17},{... | collective-permute-start | bytes 516104 | tf_op jit(solution)/shard_map/ppermute | solution.py:951
  510.4 17.8 %collective-permute-start.24 = (bf16[4,8,2688]{2,0,1:T(4,128)(2,1)S(1)}, bf16[4,8,2688]{2,0,1:T(4,128)(2,1)S(1)}, u32[]{:S(2)}, u32[]{:S(2)}) collective-permute-start(bf16[4,8,2688]{2,0,1:T(4,128)(2,1)S(1)} %pad_maximum_fusion.6), channel_id=1, source_target_pairs={{0,24},{4,28},{8,0},{12,4},{16,8},{20,12},{24,16},{28,20},{1,25},{... | collective-permute-start | bytes 516104 | tf_op jit(solution)/shard_map/ppermute | solution.py:951
  513.2 74.5 %collective-permute-start.12 = (bf16[1024,1024]{1,0:T(8,128)(2,1)}, bf16[1024,1024]{1,0:T(8,128)(2,1)}, u32[]{:S(2)}, u32[]{:S(2)}) collective-permute-start(bf16[1024,1024]{1,0:T(8,128)(2,1)} %collective-permute-done.11), channel_id=1, source_target_pairs={{0,1},{1,0},{2,3},{3,2},{4,5},{5,4},{6,7},{7,6},{8,9},{9,8},{10,11... | collective-permute-start | bytes 6291464 | tf_op jit(solution)/shard_map/ppermute | solution.py:845
  518.2 26.8 %collective-permute-start.17 = (bf16[512,1024]{1,0:T(8,128)(2,1)}, bf16[512,1024]{1,0:T(8,128)(2,1)}, u32[]{:S(2)}, u32[]{:S(2)}) collective-permute-start(bf16[512,1024]{1,0:T(8,128)(2,1)} %get-tuple-element.109), channel_id=1, source_target_pairs={{0,0},{2,4},{4,2},{6,6},{8,8},{10,12},{12,10},{14,14},{16,16},{18,... | collective-permute-start | bytes 3145736 | tf_op jit(solution)/shard_map/ppermute | solution.py:839
  527.7 52.8 %collective-permute-start.18 = (bf16[512,1024]{1,0:T(8,128)(2,1)}, bf16[512,1024]{1,0:T(8,128)(2,1)}, u32[]{:S(2)}, u32[]{:S(2)}) collective-permute-start(bf16[512,1024]{1,0:T(8,128)(2,1)} %get-tuple-element.110), channel_id=1, source_target_pairs={{0,1},{1,0},{2,5},{3,4},{4,3},{5,2},{6,7},{7,6},{8,9},{9,8},{10,13... | collective-permute-start | bytes 3145736 | tf_op jit(solution)/shard_map/ppermute | solution.py:931
  529.3 55.1 %collective-permute-start.25 = (bf16[16,8,2688]{2,0,1:T(8,128)(2,1)S(1)}, bf16[16,8,2688]{2,0,1:T(8,128)(2,1)S(1)}, u32[]{:S(2)}, u32[]{:S(2)}) collective-permute-start(bf16[16,8,2688]{2,0,1:T(8,128)(2,1)S(1)} %concatenate.107), channel_id=1, source_target_pairs={{0,4},{4,0},{8,12},{12,8},{16,20},{20,16},{24,28},{28,24},{1,5},{5... | collective-permute-start | bytes 2064392 | tf_op jit(solution)/shard_map/ppermute | solution.py:842
  (28 other events, 324.4 us)
Sparse Core Ops, SparseCore 0:
  10.3 66.6 all-gather.8
  79.2 39.9 all-gather.10
  121.5 73.6 all-gather.12
  197.2 73.1 all-gather.14

commit v2 on v1

--- a/solution.py
+++ b/solution.py
@@ -377,79 +377,589 @@
     )
 
 
+MESH = pl.DeviceIdType.MESH
+HIDDEN_BLOCK = 512
+(UP_SENT, DOWN_SENT, Z_CAME, TP_SENT, TP_CAME, OWN_SENT, OWN_CAME, NEXT_SENT, NEXT_CAME) = range(9)
+
+
+class Place:
+    def __init__(self, planes):
+        self.planes = planes
+        self.shard = lax.axis_index("shard")
+        self.z = self.shard // 2
+        self.core = self.shard % 2
+        self.ctx = lax.axis_index("ctx")
+        self.tp = lax.axis_index("tp")
+        self.has_up = self.z < planes - 1
+        self.has_down = self.z > 0
+        self.crosses = self.core != self.ctx
+        self.up = {"shard": self.shard + 2}
+        self.down = {"shard": self.shard - 2}
+        self.next_tp = {"tp": 1 - self.tp}
+        self.next_core = {"shard": 2 * self.z + 1 - self.core}
+        self.turned = {"shard": 2 * self.z + self.ctx, "ctx": self.core}
+
+    def greet(self, planes_too, turned):
+        barrier = pltpu.get_barrier_semaphore()
+        count = 2
+
+        def signal(device):
+            pl.semaphore_signal(barrier, inc=1, device_id=device, device_id_type=MESH)
+
+        signal(self.next_tp)
+        signal(self.next_core)
+        if planes_too:
+            pl.when(self.has_up)(lambda: signal(self.up))
+            pl.when(self.has_down)(lambda: signal(self.down))
+            count = count + self.has_up.astype(jnp.int32) + self.has_down.astype(jnp.int32)
+        if turned:
+            pl.when(self.crosses)(lambda: signal(self.turned))
+            count = count + self.crosses.astype(jnp.int32)
+        pl.semaphore_wait(barrier, count)
+
+
+class Flow:
+    def __init__(self, at, own, slot, sems):
+        self.at, self.own, self.slot, self.sems = at, own, slot, sems
+
+    def copy(self, kind, plane, own=False):
+        at = self.at
+        half = 1 - at.tp if kind == NEXT_SENT else at.tp
+        piece = self.slot(2 * plane + at.core, half)
+        device, came = {
+            UP_SENT: (at.up, Z_CAME),
+            DOWN_SENT: (at.down, Z_CAME),
+            TP_SENT: (at.next_tp, TP_CAME),
+            OWN_SENT: (at.next_core, OWN_CAME),
+            NEXT_SENT: (at.next_core, NEXT_CAME),
+        }[kind]
+        return pltpu.make_async_remote_copy(
+            src_ref=self.own if own else piece,
+            dst_ref=piece,
+            send_sem=self.sems.at[kind, plane],
+            recv_sem=self.sems.at[came, plane],
+            device_id=device,
+            device_id_type=MESH,
+        )
+
+    def came(self, kind, plane):
+        sent = {Z_CAME: UP_SENT, TP_CAME: TP_SENT, OWN_CAME: OWN_SENT, NEXT_CAME: NEXT_SENT}[kind]
+        at = self.at
+        shard = 2 * plane + (at.core if kind in (Z_CAME, TP_CAME) else 1 - at.core)
+        half = at.tp if kind in (Z_CAME, OWN_CAME) else 1 - at.tp
+        piece = self.slot(shard, half)
+        return pltpu.make_async_remote_copy(
+            src_ref=piece, dst_ref=piece, send_sem=self.sems.at[sent, plane],
+            recv_sem=self.sems.at[kind, plane], device_id=at.next_core, device_id_type=MESH,
+        )
+
+    def pieces(self, distance):
+        at = self.at
+        if distance == 0:
+            return [(None, at.z, True, True)]
+        return [
+            (at.z >= distance, at.z - distance, True, False),
+            (at.z < at.planes - distance, at.z + distance, False, True),
+        ]
+
+    def each(self, distance, act):
+        for there, plane, below, above in self.pieces(distance):
+            if there is None:
+                act(plane, below, above)
+            else:
+                pl.when(there)(functools.partial(act, plane, below, above))
+
+    def pass_on(self, distance, z=False, tp=False, core=False, fresh=None, wait=False):
+        own = (distance == 0) if fresh is None else fresh
+
+        def act(plane, below, above):
+            if wait:
+                self.came(Z_CAME, plane).wait_recv()
+            if z:
+                if below:
+                    pl.when(self.at.has_up)(lambda: self.copy(UP_SENT, plane, own).start())
+                if above:
+                    pl.when(self.at.has_down)(lambda: self.copy(DOWN_SENT, plane, own).start())
+            if tp:
+                self.copy(TP_SENT, plane, own).start()
+            if core:
+                self.copy(OWN_SENT, plane, own).start()
+
+        self.each(distance, act)
+
+    def sent(self, distance, z=False, tp=False, core=False):
+        def act(plane, below, above):
+            if z:
+                if below:
+                    pl.when(self.at.has_up)(lambda: self.copy(UP_SENT, plane).wait_send())
+                if above:
+                    pl.when(self.at.has_down)(lambda: self.copy(DOWN_SENT, plane).wait_send())
+            if tp:
+                self.copy(TP_SENT, plane).wait_send()
+            if core:
+                self.copy(OWN_SENT, plane).wait_send()
+
+        self.each(distance, act)
+
+    def wait(self, kind, distance):
+        self.each(distance, lambda plane, below, above: self.came(kind, plane).wait_recv())
+
+    def pass_next(self, distance, wait=True):
+        def act(plane, below, above):
+            if wait:
+                self.came(TP_CAME, plane).wait_recv()
+            self.copy(NEXT_SENT, plane).start()
+
+        self.each(distance, act)
+
+    def sent_next(self, distance):
+        self.each(distance, lambda plane, below, above: self.copy(NEXT_SENT, plane).wait_send())
+
+
+def weight_flows(at, own_o, own_e, own_r, full_o, full_e, full_r, sems, blocks):
+    flow_o = Flow(at, own_o, lambda s, h: full_o.at[s, h], sems.at[0])
+    flows = []
+    for block in range(blocks):
+        span = pl.ds(block * HIDDEN_BLOCK, HIDDEN_BLOCK)
+        flows.append(
+            [
+                Flow(at, own_e.at[:, span], lambda s, h, span=span: full_e.at[s, h, :, span], sems.at[1 + 2 * block]),
+                Flow(at, own_r.at[span, :], lambda s, h, span=span: full_r.at[s, h, span, :], sems.at[2 + 2 * block]),
+            ]
+        )
+    return flow_o, flows
+
+
+def turned_copy(at, source, target, sems):
+    return pltpu.make_async_remote_copy(
+        src_ref=source, dst_ref=target, send_sem=sems.at[0], recv_sem=sems.at[1],
+        device_id=at.turned, device_id_type=MESH,
+    )
+
+
+ROWS = 256
+
+
 def project_body(
-    side, x_ref, gain_ref, shift_ref, w_own, w_other, bias_ref, down_ref, up_ref, cos_ref, sin_ref,
-    own_q, own_k, own_v, other_q, other_k, other_v, xn_ref, u_ref,
+    planes, blocks,
+    tokens_ref, spots_ref, factors_ref, factors_next, shared_ref, offsets_ref, w_ref, own_o, own_e, own_r,
+    gain_ref, shift_ref, rates_ref,
+    x_out, factors_out, shared_out, offsets_out, w_out, full_o, full_e, full_r,
+    q_out, k_out, v_out, xn_out, u_out, cos_out, sin_out,
+    x_vm, w_vm, stage, spots_all, factors_vm, offsets_vm, jd_vm,
+    w_sems, flow_sems, x_sems, spot_sems, factor_sems, shared_sems, offset_sems, local_sems, out_sems, move_sems,
 ):
-    scaled, _ = row_norm(x_ref[...].astype(F32))
-    xn = (scaled * gain_ref[...] + shift_ref[...]).astype(B16)
-    xn_ref[...] = xn
-    u = dot(xn, down_ref[...], 1, 1).astype(B16)
-    u_ref[...] = u
-    core = side[0]
-    for w_ref, half, outs in (
-        (w_own, core, (own_q, own_k, own_v)),
-        (w_other, 1 - core, (other_q, other_k, other_v)),
-    ):
+    at = Place(planes)
+    rows_all, width = x_vm.shape
+    half = w_ref.shape[2]
+    at.greet(True, True)
+    chunks = rows_all // ROWS
+    flow = Flow(at, w_ref, lambda s, h: w_out.at[s, h], w_sems)
+    flow_o, flows = weight_flows(at, own_o, own_e, own_r, full_o, full_e, full_r, flow_sems, blocks)
+    ahead = [flow_o] + [f for pair in flows[: blocks - 1] for f in pair]
+    holds = at.core == at.ctx
+
+    def local(source, target, index):
+        return pltpu.make_async_copy(source, target, local_sems.at[index])
+
+    flow.pass_on(0, z=True, tp=True)
+
+    def x_chunk(i):
+        span = pl.ds(i * ROWS, ROWS)
+        return turned_copy(at, tokens_ref.at[at.tp, span], x_vm.at[span], x_sems.at[i])
+
+    spot_copy = turned_copy(at, spots_ref, spots_all.at[0], spot_sems.at[0])
+    spot_here = local(spots_ref, spots_all.at[0], 0)
+
+    @pl.when(at.crosses)
+    def _():
+        spot_copy.start()
+        for i in range(chunks):
+            x_chunk(i).start()
+
+    @pl.when(holds)
+    def _():
+        spot_here.start()
+        for i in range(chunks):
+            span = pl.ds(i * ROWS, ROWS)
+            local(tokens_ref.at[at.tp, span], x_vm.at[span], 1 + i).start()
+
+    flow.pass_on(0, core=True)
+
+    def remote(source, target, sems, device):
+        return pltpu.make_async_remote_copy(
+            src_ref=source, dst_ref=target, send_sem=sems.at[0], recv_sem=sems.at[1],
+            device_id=device, device_id_type=MESH,
+        )
+
+    offset_copy = remote(offsets_ref, offsets_out.at[at.tp], offset_sems, at.next_tp)
+    offset_came = remote(offsets_ref, offsets_out.at[1 - at.tp], offset_sems, at.next_tp)
+    offset_copy.start()
+    local(offsets_ref, offsets_out.at[at.tp], 1 + chunks).start()
+    next_copy = remote(factors_next, factors_out.at[at.tp], factor_sems.at[0], at.next_tp)
+    next_came = remote(factors_next, factors_out.at[1 - at.tp], factor_sems.at[0], at.next_tp)
+    own_factors = remote(factors_ref, factors_out.at[at.tp], factor_sems.at[1], at.next_core)
+    shared_copy = remote(shared_ref, shared_out, shared_sems, at.next_core)
+    next_factors = remote(factors_out.at[1 - at.tp], factors_out.at[1 - at.tp], factor_sems.at[2], at.next_core)
+
+    @pl.when(holds)
+    def _():
+        next_copy.start()
+        own_factors.start()
+        shared_copy.start()
+        local(factors_ref, factors_out.at[at.tp], 2 + chunks).start()
+        local(shared_ref, shared_out, 3 + chunks).start()
+
+    local(w_ref, w_out.at[at.shard, at.tp], 4 + chunks).start()
+    local(own_o, full_o.at[at.shard, at.tp], 5 + chunks).start()
+    local(own_e, full_e.at[at.shard, at.tp], 6 + chunks).start()
+    local(own_r, full_r.at[at.shard, at.tp], 7 + chunks).start()
+
+    @pl.when(at.crosses)
+    def _():
+        spot_copy.wait_recv()
+
+    @pl.when(holds)
+    def _():
+        spot_here.wait()
+
+    spot_next = remote(spots_all.at[0], spots_all.at[1], spot_sems.at[1], at.next_core)
+    spot_next.start()
+
+    @pl.when(holds)
+    def _():
+        next_came.wait_recv()
+        next_factors.start()
+
+    lane = lax.broadcasted_iota(jnp.int32, (1, 128), 1) % 64
+    turned = lane < 60
+    early = lane % 20 < 10
+
+    def tables(part):
+        def body(i, carry):
+            span = pl.ds(pl.multiple_of(i * ROWS, ROWS), ROWS)
+            angle = dot(spots_all[part, :, span], rates_ref[...], 0, 0)
+            out = pl.ds(pl.multiple_of(part * rows_all + i * ROWS, ROWS), ROWS)
+            cos_out[out, :] = jnp.where(turned, jnp.cos(angle), 1.0)
+            sine = jnp.sin(angle)
+            sin_out[out, :] = jnp.where(turned, jnp.where(early, -sine, sine), 0.0)
+            return carry
+
+        lax.fori_loop(0, chunks, body, 0)
+
+    tables(0)
+    flow.pass_on(1, z=True, tp=True, core=True, wait=True)
+    spot_next.wait()
+    tables(1)
+
+    @pl.when(holds)
+    def _():
+        local(factors_ref, factors_out.at[at.tp], 2 + chunks).wait()
+        local(shared_ref, shared_out, 3 + chunks).wait()
+        own_factors.wait_send()
+        shared_copy.wait_send()
+        next_copy.wait_send()
+        next_factors.wait_send()
+
+    @pl.when(at.crosses)
+    def _():
+        own_factors.wait_recv()
+        shared_copy.wait_recv()
+        remote(factors_out.at[1 - at.tp], factors_out.at[1 - at.tp], factor_sems.at[2], at.next_core).wait_recv()
+
+    offset_copy.wait_send()
+    offset_came.wait_recv()
+    local(offsets_ref, offsets_out.at[at.tp], 1 + chunks).wait()
+    loads = [
+        pltpu.make_async_copy(factors_out, factors_vm, out_sems.at[0]),
+        pltpu.make_async_copy(offsets_out, offsets_vm, out_sems.at[1]),
+        pltpu.make_async_copy(shared_out.at[:, pl.ds(0, width)], jd_vm, out_sems.at[2]),
+    ]
+    for load in loads:
+        load.start()
+    if planes > 2:
+        flow.pass_on(2, z=True, tp=True, core=True, wait=True)
+    for load in loads:
+        load.wait()
+
+    kept = []
+
+    def x_ready(i):
+        span = pl.ds(i * ROWS, ROWS)
+
+        @pl.when(at.crosses)
+        def _():
+            x_chunk(i).wait()
+
+        @pl.when(holds)
+        def _():
+            local(tokens_ref.at[at.tp, span], x_vm.at[span], 1 + i).wait()
+
+        keep = pltpu.make_async_copy(x_vm.at[span], x_out.at[span], x_sems.at[i, 2])
+        keep.start()
+        kept.append(keep)
+        scaled, _ = row_norm(x_vm[span, :].astype(F32))
+        xn = (scaled * gain_ref[...] + shift_ref[...]).astype(B16)
+        xn_out[span, :] = xn
+        u_out[span, :] = dot(xn, jd_vm[...], 1, 1).astype(B16)
+
+    for i in range(chunks // 2):
+        x_ready(i)
+    for far in range(3, planes):
+        flow.pass_on(far, z=True, tp=True, core=True, wait=True)
+    for other in ahead:
+        other.pass_on(0, z=True)
+    for i in range(chunks // 2, chunks):
+        x_ready(i)
+
+    outs = (q_out, k_out, v_out)
+    sending = []
+
+    def compute(order, owner):
         for part in range(3):
-            w = w_ref[:, 0, part].reshape(-1, w_ref.shape[-1])
-            value = dot(xn, w) + bias_ref[half, part] + dot(u, up_ref[half, part])
-            if part == 2:
-                outs[2][...] = value.astype(B16)
-                continue
-            for at in range(0, value.shape[1], 128):
-                piece = value[:, at : at + 128]
-                outs[part][:, at : at + 128] = (
-                    piece * cos_ref[...] + partner(piece) * sin_ref[...]
-                ).astype(B16)
-
-
-def project(side, x, gain, shift, weight, bias, down, up, cosine, sine):
-    rows, width = x.shape
-    shards_, _, _, depth, half = weight.shape
-    block = 256
-    row = lambda columns: pl.BlockSpec((block, columns), lambda i, s: (i, 0))
-    whole = lambda shape: pl.BlockSpec(shape, lambda i, s: (0,) * len(shape))
-    w_spec = lambda pick: pl.BlockSpec(
-        (shards_, 1, 3, depth, half), lambda i, s: (0, pick(s[0]), 0, 0, 0)
-    )
-    part = jax.ShapeDtypeStruct((rows, half), B16)
+            load = pltpu.make_async_copy(w_out.at[:, owner, part], w_vm.at[part], out_sems.at[part])
+            load.start()
+        for part in range(3):
+            pltpu.make_async_copy(w_out.at[:, owner, part], w_vm.at[part], out_sems.at[part]).wait()
+            w = w_vm[part].reshape(width, half)
+            bias = offsets_vm[owner, :, part * half : (part + 1) * half]
+            up = factors_vm[owner, :, part * half : (part + 1) * half]
+
+            def body(i, carry):
+                span = pl.ds(pl.multiple_of(i * ROWS, ROWS), ROWS)
+                value = dot(xn_out[span, :], w) + bias + dot(u_out[span, :], up)
+                if part == 2:
+                    stage[order, part, span, :] = value.astype(B16)
+                else:
+                    for col in range(0, half, 128):
+                        piece = value[:, col : col + 128]
+                        stage[order, part, span, col : col + 128] = (
+                            piece * cos_out[span, :] + partner(piece) * sin_out[span, :]
+                        ).astype(B16)
+                return carry
+
+            lax.fori_loop(0, chunks, body, 0)
+
+            def moves(part=part):
+                here = pltpu.make_async_copy(
+                    stage.at[order, part], outs[part].at[pl.ds(0, rows_all)], out_sems.at[3 + part]
+                )
+                there = remote(
+                    stage.at[order, part], outs[part].at[pl.ds(rows_all, rows_all)],
+                    move_sems.at[part], at.next_core,
+                )
+                return here, there
+
+            @pl.when(owner == at.core)
+            def _():
+                moves()[0].start()
+
+            @pl.when(owner != at.core)
+            def _():
+                moves()[1].start()
+
+            sending.append((owner, moves))
+
+    for far in range(planes):
+        flow.wait(OWN_CAME, far)
+    local(w_ref, w_out.at[at.shard, at.tp], 4 + chunks).wait()
+    for far in range(planes - 1):
+        flow.pass_next(far)
+    compute(0, at.tp)
+    flow.pass_next(planes - 1)
+    for far in range(planes):
+        flow.wait(NEXT_CAME, far)
+    compute(1, 1 - at.tp)
+
+    for keep in kept:
+        keep.wait()
+    for other in ahead:
+        other.wait(Z_CAME, 1)
+        other.sent(0, z=True)
+    for far in range(planes):
+        flow.sent(far, z=True, tp=True, core=True)
+        flow.sent_next(far)
+    for i in range(3):
+        local((own_o, own_e, own_r)[i], (full_o, full_e, full_r)[i].at[at.shard, at.tp], 5 + i + chunks).wait()
+
+    @pl.when(at.crosses)
+    def _():
+        spot_copy.wait_send()
+
+    for owner, moves in sending:
+
+        @pl.when(owner == at.core)
+        def _():
+            moves()[0].wait()
+
+        @pl.when(owner != at.core)
+        def _():
+            moves()[1].wait_send()
+
+    for _, moves in sending[:3]:
+        moves()[1].wait_recv()
+
+
+def project(planes, tokens, spots, factors, factors_next, shared, offsets, weight, own_o, own_e, own_r, gain, shift, rates):
+    rows, width = tokens.shape[1:]
+    _, depth, half = weight.shape
+    rank = factors.shape[0]
+    blocks = own_e.shape[1] // HIDDEN_BLOCK
+    chunks = rows // ROWS
+    shape = jax.ShapeDtypeStruct
+    hbm = pl.BlockSpec(memory_space=pl.ANY)
+    vmem = pl.BlockSpec(memory_space=pltpu.VMEM)
+    dma = pltpu.SemaphoreType.DMA
     return pl.pallas_call(
-        project_body,
-        grid_spec=pltpu.PrefetchScalarGridSpec(
-            num_scalar_prefetch=1,
-            grid=(rows // block,),
-            in_specs=[
-                row(width), whole((1, width)), whole((1, width)),
-                w_spec(lambda s: s), w_spec(lambda s: 1 - s),
-                whole(bias.shape), whole(down.shape), whole(up.shape), row(128), row(128),
-            ],
-            out_specs=[row(half)] * 6 + [row(width), row(down.shape[0])],
+        functools.partial(project_body, planes, blocks),
+        in_specs=[hbm] * 1 + [vmem] * 12,
+        out_specs=[hbm] * 11 + [vmem] * 4,
+        out_shape=[
+            shape((rows, width), B16),
+            shape((2,) + factors.shape, B16),
+            shape(shared.shape, B16),
+            shape((2,) + offsets.shape, F32),
+            shape((2 * planes, 2) + weight.shape, B16),
+            shape((2 * planes, 2) + own_o.shape, B16),
+            shape((2 * planes, 2) + own_e.shape, B16),
+            shape((2 * planes, 2) + own_r.shape, B16),
+            shape((2 * rows, half), B16),
+            shape((2 * rows, half), B16),
+            shape((2 * rows, half), B16),
+            shape((rows, width), B16),
+            shape((rows, rank), B16),
+            shape((2 * rows, 128), F32),
+            shape((2 * rows, 128), F32),
+        ],
+        scratch_shapes=[
+            pltpu.VMEM((rows, width), B16),
+            pltpu.VMEM((3, 2 * planes, depth, half), B16),
+            pltpu.VMEM((2, 3, rows, half), B16),
+            pltpu.VMEM((2,) + spots.shape, B16),
+            pltpu.VMEM((2,) + factors.shape, B16),
+            pltpu.VMEM((2,) + offsets.shape, F32),
+            pltpu.VMEM((rank, width), B16),
+            dma((9, planes)),
+            dma((1 + 2 * blocks, 9, planes)),
+            dma((chunks, 3)),
+            dma((2, 2)),
+            dma((3, 2)),
+            dma((2,)),
+            dma((2,)),
+            dma((8 + chunks,)),
+            dma((6,)),
+            dma((3, 2)),
+        ],
+        compiler_params=pltpu.CompilerParams(
+            vmem_limit_bytes=VMEM_LIMIT, collective_id=0, has_side_effects=True
         ),
-        out_shape=[part] * 6
-        + [
-            jax.ShapeDtypeStruct((rows, width), B16),
-            jax.ShapeDtypeStruct((rows, down.shape[0]), B16),
-        ],
-        compiler_params=params(),
         cost_estimate=pl.CostEstimate(
-            flops=2 * rows * width * 6 * half, bytes_accessed=16 * 2**20, transcendentals=0
+            flops=2 * rows * width * 6 * half, bytes_accessed=100 * 2**20, transcendentals=0
         ),
-    )(side, x, gain, shift, weight, weight, bias, down, up, cosine, sine)
-
-
-def attend_body(q_ref, k_ref, v_ref, o_ref, inv_ref, e_ref, vm_ref):
+    )(tokens, spots, factors, factors_next, shared, offsets, weight, own_o, own_e, own_r, gain, shift, rates)
+
+
+def attend_body(
+    planes, blocks,
+    q_ref, k_ref, v_ref, cot_ref, own_o, own_e, own_r, in_o, in_e, in_r,
+    o_ref, inv_ref, e_ref, o_next, cot_out, full_o, full_e, full_r,
+    vm_ref, stage, cot_vm, flow_sems, stage_sems, cot_sems,
+):
+    at = Place(planes)
     rows_all, length = q_ref.shape[0], k_ref.shape[0]
     low = low_lanes()
-
-    @pl.when(pl.program_id(1) == 0)
+    pair, turn = pl.program_id(0), pl.program_id(1)
+    turns = length // rows_all
+    now = pair * turns + turn
+    pairs = stage.shape[0] // (turns // 2)
+    count = pairs * turns
+    flow_o, flows = weight_flows(at, own_o, own_e, own_r, full_o, full_e, full_r, flow_sems, blocks)
+    zero = [flow_o] + flows[0]
+    last = planes - 1
+    cot_move = turned_copy(at, cot_ref.at[at.tp], cot_out, cot_sems)
+    cot_load = pltpu.make_async_copy(cot_ref.at[at.tp], cot_vm, cot_sems.at[2])
+    cot_keep = pltpu.make_async_copy(cot_vm, cot_out, cot_sems.at[3])
+
+    def when(step, act):
+        pl.when(now == min(step * count // 16, count - 1))(act)
+
+    @pl.when(now == 0)
+    def _():
+        at.greet(True, True)
+        for flow in zero:
+            flow.pass_on(1, z=True, tp=True, core=True)
+            flow.pass_on(0, tp=True, core=True)
+        for flow in flows[1]:
+            flow.pass_on(1, z=True, core=True)
+        pl.when(at.crosses)(lambda: cot_move.start())
+        pl.when(jnp.logical_not(at.crosses))(lambda: cot_load.start())
+        for flow in flows[1] + flows[2]:
+            flow.pass_on(0, core=True)
+
+    def at_3():
+        @pl.when(jnp.logical_not(at.crosses))
+        def _():
+            cot_load.wait()
+            cot_keep.start()
+
+        for flow in zero:
+            flow.pass_on(2, z=True, tp=True, core=True, wait=True)
+
+    def at_4():
+        for flow in flows[2]:
+            flow.pass_on(1, z=True, core=True)
+
+    def at_5():
+        for flow in flows[1]:
+            flow.pass_on(2, z=True, core=True, wait=True)
+
+    def at_7():
+        for flow in zero:
+            flow.pass_on(3, tp=True, core=True, wait=True)
+        for flow in flows[1]:
+            flow.pass_on(0, tp=True)
+            flow.pass_on(1, tp=True)
+            flow.pass_on(2, tp=True)
+        for flow in zero:
+            flow.pass_next(0)
+            flow.pass_next(1)
+
+    def at_8():
+        for flow in flows[2]:
+            flow.pass_on(2, z=True, core=True, wait=True)
+        for flow in flows[3]:
+            flow.pass_on(0, z=True)
+
+    def at_10():
+        for flow in flows[1]:
+            flow.pass_on(3, tp=True, core=True, wait=True)
+        for flow in zero:
+            flow.pass_next(2)
+            flow.pass_next(3)
+
+    def at_12():
+        for flow in flows[2]:
+            flow.pass_on(3, core=True, wait=True)
+
+    def at_13():
+        for flow in flows[3]:
+            flow.pass_on(1, z=True, wait=True)
+
+    def at_15():
+        for flow in flows[3]:
+            flow.pass_on(2, z=True, wait=True)
+
+    for step, act in ((3, at_3), (4, at_4), (5, at_5), (7, at_7), (8, at_8), (10, at_10), (12, at_12), (13, at_13), (15, at_15)):
+        when(step, act)
+
+    @pl.when(turn == 0)
     def _():
         vm_ref[0] = jnp.where(low, v_ref[...], 1).astype(B16)
         vm_ref[1] = jnp.where(low, 1, v_ref[...]).astype(B16)
 
     step = min(256, rows_all)
-    for at in range(0, rows_all, step):
-        rows = pl.ds(at, step)
+    for begin in range(0, rows_all, step):
+        rows = pl.ds(begin, step)
         q = q_ref[rows, :]
         sums = []
         for head in range(2):
@@ -464,30 +974,101 @@
         o_ref[rows, :] = (jnp.where(low, sums[0], sums[1]) * inverse).astype(B16)
         inv_ref[rows, :] = inverse
 
-
-def attend(query, key, value):
+    def o_move(index):
+        per = turns // 2
+        rows = pl.ds(pl.multiple_of(index % per * rows_all, rows_all), rows_all)
+        columns = pl.ds(pl.multiple_of(index // per * 128, 128), 128)
+        return pltpu.make_async_remote_copy(
+            src_ref=stage.at[index], dst_ref=o_next.at[rows, columns],
+            send_sem=stage_sems.at[0, index], recv_sem=stage_sems.at[1, index],
+            device_id=at.next_core, device_id_type=MESH,
+        )
+
+    @pl.when(turn >= turns // 2)
+    def _():
+        index = pair * (turns // 2) + turn - turns // 2
+        stage[index] = o_ref[...]
+        o_move(index).start()
+
+    @pl.when(now == count - 1)
+    def _():
+        for flow in flows[3]:
+            flow.wait(Z_CAME, 3)
+        for flow in zero + flows[1] + flows[2]:
+            for far in range(planes):
+                flow.wait(OWN_CAME, far)
+        for flow in zero:
+            for far in range(planes):
+                flow.wait(NEXT_CAME, far)
+                flow.sent_next(far)
+        for flow in flows[1]:
+            for far in range(planes):
+                flow.wait(TP_CAME, far)
+        for flow in zero + flows[1] + flows[2] + flows[3]:
+            for far in range(planes):
+                moved = flow in flows[3]
+                flow.sent(
+                    far,
+                    z=(far < last) and (moved or far > 0),
+                    tp=flow in zero or flow in flows[1],
+                    core=not moved,
+                )
+
+        @pl.when(at.crosses)
+        def _():
+            cot_move.wait()
+
+        @pl.when(jnp.logical_not(at.crosses))
+        def _():
+            cot_keep.wait()
+
+        for index in range(count // 2):
+            o_move(index).wait()
+
+
+def attend(planes, query, key, value, cotangent, own_o, own_e, own_r, full_o, full_e, full_r):
     length, width = query.shape
-    block = min(1024, length)
+    block = min(512, length // 2)
+    blocks = own_e.shape[1] // HIDDEN_BLOCK
+    turns = length // block
+    pairs = width // 128
     rows = pl.BlockSpec((block, 128), lambda p, i: (i, p))
     full = pl.BlockSpec((length, 128), lambda p, i: (0, p))
+    hbm = pl.BlockSpec(memory_space=pl.ANY)
+    shape = jax.ShapeDtypeStruct
+    like = lambda array: shape(array.shape, array.dtype)
+    dma = pltpu.SemaphoreType.DMA
     return pl.pallas_call(
-        attend_body,
-        grid=(width // 128, length // block),
-        in_specs=[rows, full, full],
-        out_specs=[rows, rows, pl.BlockSpec((2, block, length), lambda p, i: (p, i, 0))],
+        functools.partial(attend_body, planes, blocks),
+        grid=(pairs, turns),
+        in_specs=[rows, full, full] + [hbm] * 7,
+        out_specs=[rows, rows, pl.BlockSpec((2, block, length), lambda p, i: (p, i, 0))] + [hbm] * 5,
         out_shape=[
-            jax.ShapeDtypeStruct((length, width), B16),
-            jax.ShapeDtypeStruct((length, width), F32),
-            jax.ShapeDtypeStruct((width // 64, length, length), B16),
+            shape((length, width), B16),
+            shape((length, width), F32),
+            shape((width // 64, length, length), B16),
+            shape((length // 2, width), B16),
+            shape(cotangent.shape[1:], B16),
+            like(full_o), like(full_e), like(full_r),
         ],
-        scratch_shapes=[pltpu.VMEM((2, length, 128), B16)],
-        compiler_params=params(),
+        input_output_aliases={7: 5, 8: 6, 9: 7},
+        scratch_shapes=[
+            pltpu.VMEM((2, length, 128), B16),
+            pltpu.VMEM((pairs * turns // 2, block, 128), B16),
+            pltpu.VMEM(cotangent.shape[1:], B16),
+            dma((1 + 2 * blocks, 9, planes)),
+            dma((2, pairs * turns // 2)),
+            dma((4,)),
+        ],
+        compiler_params=pltpu.CompilerParams(
+            vmem_limit_bytes=VMEM_LIMIT, collective_id=1, has_side_effects=True
+        ),
         cost_estimate=pl.CostEstimate(
             flops=16 * length * length * width,
             bytes_accessed=width // 64 * length * length * 2,
             transcendentals=width // 64 * length * length,
         ),
-    )(query, key, value)
+    )(query, key, value, cotangent, own_o, own_e, own_r, full_o, full_e, full_r)
 
 
 def attend_back_body(
@@ -574,54 +1155,140 @@
 
 
 def middle_body(
-    side, x_ref, cot_ref, own_ref, other_ref, wo_ref, e_ref, r_ref,
-    out_off, gain_ref, shift_ref, wide_off, shrink_off,
-    od_ref, ou_ref, ed_ref, ru_ref, eu_ref, rd_ref,
-    output_ref, gh_ref, gown_ref, gother_ref,
-    t_od, t_ou, t_ed, t_ru, t_eu, t_rd,
+    planes, blocks,
+    x_ref, cot_ref, own_ref, other_ref, wo_ref, factors_ref, shared_ref, offsets_ref,
+    out_off, gain_ref, shift_ref, shrink_off, in_e, in_r,
+    output_ref, gh_ref, t_od, t_ou, t_ed, t_ru, t_eu, t_rd, gatt_out, full_e, full_r,
     hidden, xn_ref, total, back, u2_ref, u3_ref, u4_sum, g4_ref, g3_sum,
+    e_vm, r_vm, gown_vm, gother_vm, load_sems, flow_sems, grad_sems,
 ):
+    at = Place(planes)
     f = pl.program_id(0)
-    last = pl.num_programs(0) - 1
-    core = side[0]
-    rows_all = x_ref.shape[0]
+    last = 2 * blocks - 1
+    core = at.core
+    rows_all, width = x_ref.shape
+    half = own_ref.shape[1]
+    hidden_half = blocks * HIDDEN_BLOCK
     step = 256
-
-    def wo_half(half):
-        w = wo_ref[:, half]
+    flows = []
+    for block in range(blocks):
+        span = pl.ds(block * HIDDEN_BLOCK, HIDDEN_BLOCK)
+        flows.append(
+            [
+                Flow(at, None, lambda s, h, span=span: full_e.at[s, h, :, span], flow_sems.at[2 * block]),
+                Flow(at, None, lambda s, h, span=span: full_r.at[s, h, span, :], flow_sems.at[2 * block + 1]),
+            ]
+        )
+    planes_all = range(planes)
+
+    def pass_on(pair, **how):
+        for flow in pair:
+            for far in planes_all:
+                flow.pass_on(far, fresh=False, **how)
+
+    def pass_next(pair, wait):
+        for flow in pair:
+            for far in planes_all:
+                flow.pass_next(far, wait)
+
+    def arrived(pair, kind):
+        for flow in pair:
+            for far in planes_all:
+                flow.wait(kind, far)
+
+    def loads(index, slot):
+        tp_half = jnp.where(index < blocks, at.tp, 1 - at.tp)
+        span = pl.ds(pl.multiple_of(index % blocks * HIDDEN_BLOCK, HIDDEN_BLOCK), HIDDEN_BLOCK)
+        return (
+            pltpu.make_async_copy(full_e.at[:, tp_half, :, span], e_vm.at[slot], load_sems.at[0, slot]),
+            pltpu.make_async_copy(full_r.at[:, tp_half, span, :], r_vm.at[slot], load_sems.at[1, slot]),
+        )
+
+    def wo_half(part):
+        w = wo_ref[:, part]
         return jnp.concatenate([w[i] for i in range(w.shape[0])], axis=1)
 
+    jd, ed, ou, ru = (pl.ds(i * width, width) for i in range(4))
+    od = pl.ds(3 * half, half)
+
     @pl.when(f == 0)
     def _():
+        for load in loads(0, 0):
+            load.start()
+        at.greet(False, False)
+        pass_on(flows[2], tp=True)
+        pass_on(flows[3], core=True)
+        pass_next(flows[1], False)
         w_own, w_other = wo_half(core), wo_half(1 - core)
-        for at in range(0, rows_all, step):
-            rows = pl.ds(at, step)
+        for begin in range(0, rows_all, step):
+            rows = pl.ds(begin, step)
             own, other = own_ref[rows, :], other_ref[rows, :]
-            u2 = (dot(own, od_ref[core], 1, 1) + dot(other, od_ref[1 - core], 1, 1)).astype(B16)
+            u2 = (
+                dot(own, factors_ref[core, :, od], 1, 1) + dot(other, factors_ref[1 - core, :, od], 1, 1)
+            ).astype(B16)
             u2_ref[rows, :] = u2
             h = (
                 x_ref[rows, :].astype(F32) + dot(own, w_own) + dot(other, w_other)
-                + out_off[...] + dot(u2, ou_ref[...])
+                + out_off[...] + dot(u2, shared_ref[:, ou])
             )
             hidden[rows, :] = h
             scaled, _ = row_norm(h)
             xn = (scaled * gain_ref[...] + shift_ref[...]).astype(B16)
             xn_ref[rows, :] = xn
-            u3_ref[rows, :] = dot(xn, ed_ref[...], 1, 1).astype(B16)
-            g4_ref[rows, :] = dot(cot_ref[rows, :], ru_ref[...], 1, 1).astype(B16)
+            u3_ref[rows, :] = dot(xn, shared_ref[:, ed], 1, 1).astype(B16)
+            g4_ref[rows, :] = dot(cot_ref[rows, :], shared_ref[:, ru], 1, 1).astype(B16)
             total[rows, :] = h + shrink_off[...]
             back[rows, :] = jnp.zeros_like(h)
             u4_sum[rows, :] = jnp.zeros((step, u4_sum.shape[1]), F32)
             g3_sum[rows, :] = jnp.zeros((step, g3_sum.shape[1]), F32)
 
-    w_e = e_ref[:, 0].reshape(-1, e_ref.shape[-1])
-    w_r = jnp.concatenate([r_ref[i, 0] for i in range(r_ref.shape[0])], axis=1)
-    eu, rd = eu_ref[0], rd_ref[0]
+    @pl.when(f == 2)
+    def _():
+        pass_on(flows[3], tp=True)
+        arrived(flows[3], OWN_CAME)
+
+    @pl.when(f == 3)
+    def _():
+        pass_next(flows[2], True)
+
+    @pl.when(f == 4)
+    def _():
+        arrived(flows[1], NEXT_CAME)
+
+    @pl.when(f == 5)
+    def _():
+        pass_next(flows[3], True)
+        arrived(flows[2], NEXT_CAME)
+
+    @pl.when(f == 6)
+    def _():
+        arrived(flows[3], NEXT_CAME)
+
+    slot = f % 2
+
+    @pl.when(f < last)
+    def _():
+        for load in loads(f + 1, 1 - slot):
+            load.start()
+
+    for load in loads(f, slot):
+        load.wait()
+    tp_half = jnp.where(f < blocks, at.tp, 1 - at.tp)
+    begin_block = f % blocks * HIDDEN_BLOCK
+
+    def block_of(first):
+        return pl.ds(pl.multiple_of(first + begin_block, 128), HIDDEN_BLOCK)
+
+    w_e = e_vm[slot].reshape(width, HIDDEN_BLOCK)
+    w_r = jnp.concatenate([r_vm[slot, i] for i in range(2 * planes)], axis=1)
+    eu = factors_ref[tp_half, :, block_of(4 * half)]
+    rd = factors_ref[tp_half, :, block_of(4 * half + hidden_half)]
+    wide_off = offsets_ref[tp_half, :, block_of(3 * half)]
     sum_eu, sum_rd = 0.0, 0.0
-    for at in range(0, rows_all, step):
-        rows = pl.ds(at, step)
+    for begin in range(0, rows_all, step):
+        rows = pl.ds(begin, step)
         u3, g4 = u3_ref[rows, :], g4_ref[rows, :]
-        z = dot(xn_ref[rows, :], w_e) + wide_off[...] + dot(u3, eu)
+        z = dot(xn_ref[rows, :], w_e) + wide_off + dot(u3, eu)
         gact = dot(cot_ref[rows, :], w_r, 1, 1) + dot(g4, rd)
         cdf, density = gauss_parts(z)
         act = (z * cdf).astype(B16)
@@ -632,102 +1299,116 @@
         g3_sum[rows, :] += dot(gz, eu, 1, 1)
         sum_rd += dot(g4, act, 0, 0)
         sum_eu += dot(u3, gz, 0, 0)
-    t_rd[0] = sum_rd
-    t_eu[0] = sum_eu
+    t_rd[tp_half, :, block_of(0)] = sum_rd
+    t_eu[tp_half, :, block_of(0)] = sum_eu
 
     @pl.when(f == last)
     def _():
         w_own, w_other = wo_half(core), wo_half(1 - core)
         s_ru, s_ed, s_ou, s_own, s_other = 0.0, 0.0, 0.0, 0.0, 0.0
-        for at in range(0, rows_all, step):
-            rows = pl.ds(at, step)
+        moves = []
+        for index, begin in enumerate(range(0, rows_all, step)):
+            rows = pl.ds(begin, step)
             cot = cot_ref[rows, :]
             u4 = u4_sum[rows, :].astype(B16)
-            output_ref[rows, :] = (total[rows, :] + dot(u4, ru_ref[...])).astype(B16)
+            output_ref[rows, :] = (total[rows, :] + dot(u4, shared_ref[:, ru])).astype(B16)
             s_ru += dot(u4, cot, 0, 0)
             g3 = g3_sum[rows, :].astype(B16)
             s_ed += dot(g3, xn_ref[rows, :], 0, 0)
-            gx = back[rows, :] + dot(g3, ed_ref[...])
+            gx = back[rows, :] + dot(g3, shared_ref[:, ed])
             scaled, inverse = row_norm(hidden[rows, :])
             gh = cot.astype(F32) + back_norm(gx * gain_ref[...], scaled, inverse)
             gh_ref[rows, :] = gh
             gb = gh.astype(B16)
             s_ou += dot(u2_ref[rows, :], gb, 0, 0)
-            g2 = dot(gb, ou_ref[...], 1, 1).astype(B16)
+            g2 = dot(gb, shared_ref[:, ou], 1, 1).astype(B16)
             s_own += dot(g2, own_ref[rows, :], 0, 0)
             s_other += dot(g2, other_ref[rows, :], 0, 0)
-            gown_ref[rows, :] = (dot(gb, w_own, 1, 1) + dot(g2, od_ref[core])).astype(B16)
-            gother_ref[rows, :] = (dot(gb, w_other, 1, 1) + dot(g2, od_ref[1 - core])).astype(B16)
+            gother_vm[rows, :] = (
+                dot(gb, w_other, 1, 1) + dot(g2, factors_ref[1 - core, :, od])
+            ).astype(B16)
+            there = pltpu.make_async_remote_copy(
+                src_ref=gother_vm.at[rows], dst_ref=gatt_out.at[pl.ds(rows_all + begin, step)],
+                send_sem=grad_sems.at[0, index], recv_sem=grad_sems.at[1, index],
+                device_id=at.next_core, device_id_type=MESH,
+            )
+            there.start()
+            gown_vm[rows, :] = (dot(gb, w_own, 1, 1) + dot(g2, factors_ref[core, :, od])).astype(B16)
+            here = pltpu.make_async_copy(gown_vm.at[rows], gatt_out.at[rows], grad_sems.at[2, index])
+            here.start()
+            moves += [there, here]
         t_ru[...] = s_ru
         t_ed[...] = s_ed
         t_ou[...] = s_ou
         t_od[core] = s_own
         t_od[1 - core] = s_other
+        for pair in (flows[2], flows[3]):
+            for flow in pair:
+                for far in planes_all:
+                    flow.sent(far, tp=True, core=pair is flows[3])
+                    flow.sent_next(far)
+        for flow in flows[1]:
+            for far in planes_all:
+                flow.sent_next(far)
+        for move in moves:
+            move.wait()
 
 
 def middle(
-    side, x, cot, own, other, w_o, w_e, w_r, out_off, gain, shift, wide_off, shrink_off,
-    od, ou, ed, ru, eu, rd,
+    planes, x, cot, attended, other, w_o, factors, shared, offsets, out_off, gain, shift, shrink_off, w_e, w_r
 ):
     rows, width = x.shape
-    half = own.shape[1]
+    half = attended.shape[1]
     shards_, _, depth, hidden_half = w_e.shape
-    rank = ou.shape[0]
-    block = 512
-    per = hidden_half // block
-    steps = 2 * per
+    rank = factors.shape[1]
+    blocks = hidden_half // HIDDEN_BLOCK
     one = lambda shape: pl.BlockSpec(
-        shape, lambda f, s: (0,) * len(shape), pipeline_mode=pl.Buffered(1)
-    )
-    small = pl.BlockSpec((1, rank, block), lambda f, s: (f // per, 0, f % per))
-    full_t = jax.ShapeDtypeStruct((rank, width), F32)
-    split_t = jax.ShapeDtypeStruct((2, rank, hidden_half), F32)
+        shape, lambda f: (0,) * len(shape), pipeline_mode=pl.Buffered(1)
+    )
+    hbm = pl.BlockSpec(memory_space=pl.ANY)
+    shape = jax.ShapeDtypeStruct
+    dma = pltpu.SemaphoreType.DMA
+    chunks = rows // 256
     return pl.pallas_call(
-        middle_body,
-        grid_spec=pltpu.PrefetchScalarGridSpec(
-            num_scalar_prefetch=1,
-            grid=(steps,),
-            in_specs=[
-                one((rows, width)), one((rows, width)), one((rows, half)), one((rows, half)),
-                one(w_o.shape),
-                pl.BlockSpec((shards_, 1, depth, block), lambda f, s: (0, f // per, 0, f % per)),
-                pl.BlockSpec((shards_, 1, block, w_r.shape[3]), lambda f, s: (0, f // per, f % per, 0)),
-                one((1, width)), one((1, width)), one((1, width)),
-                pl.BlockSpec((1, block), lambda f, s: (0, f)),
-                one((1, width)),
-                one(od.shape), one(ou.shape), one(ed.shape), one(ru.shape), small, small,
-            ],
-            out_specs=[
-                one((rows, width)), one((rows, width)), one((rows, half)), one((rows, half)),
-                one((2, rank, half)), one((rank, width)), one((rank, width)), one((rank, width)),
-                small, small,
-            ],
-            scratch_shapes=[
-                pltpu.VMEM((rows, width), F32), pltpu.VMEM((rows, width), B16),
-                pltpu.VMEM((rows, width), F32), pltpu.VMEM((rows, width), F32),
-                pltpu.VMEM((rows, rank), B16), pltpu.VMEM((rows, rank), B16),
-                pltpu.VMEM((rows, rank), F32), pltpu.VMEM((rows, rank), B16),
-                pltpu.VMEM((rows, rank), F32),
-            ],
+        functools.partial(middle_body, planes, blocks),
+        grid=(2 * blocks,),
+        in_specs=[
+            one((rows, width)), one((rows, width)), one((rows, half)), one((rows, half)),
+            one(w_o.shape), one(factors.shape), one(shared.shape), one(offsets.shape),
+            one((1, width)), one((1, width)), one((1, width)), one((1, width)), hbm, hbm,
+        ],
+        out_specs=[
+            one((rows, width)), one((rows, width)),
+            one((2, rank, half)), one((rank, width)), one((rank, width)), one((rank, width)),
+            one((2, rank, hidden_half)), one((2, rank, hidden_half)), hbm, hbm, hbm,
+        ],
+        out_shape=[
+            shape((rows, width), B16), shape((rows, width), F32),
+            shape((2, rank, half), F32), shape((rank, width), F32), shape((rank, width), F32),
+            shape((rank, width), F32), shape((2, rank, hidden_half), F32), shape((2, rank, hidden_half), F32),
+            shape((2 * rows, half), B16), shape(w_e.shape, B16), shape(w_r.shape, B16),
+        ],
+        input_output_aliases={12: 9, 13: 10},
+        scratch_shapes=[
+            pltpu.VMEM((rows, width), F32), pltpu.VMEM((rows, width), B16),
+            pltpu.VMEM((rows, width), F32), pltpu.VMEM((rows, width), F32),
+            pltpu.VMEM((rows, rank), B16), pltpu.VMEM((rows, rank), B16),
+            pltpu.VMEM((rows, rank), F32), pltpu.VMEM((rows, rank), B16),
+            pltpu.VMEM((rows, rank), F32),
+            pltpu.VMEM((2, shards_, depth, HIDDEN_BLOCK), B16),
+            pltpu.VMEM((2, shards_, HIDDEN_BLOCK, w_r.shape[3]), B16),
+            pltpu.VMEM((rows, half), B16), pltpu.VMEM((rows, half), B16),
+            dma((2, 2)), dma((2 * blocks, 9, planes)), dma((3, chunks)),
+        ],
+        compiler_params=pltpu.CompilerParams(
+            vmem_limit_bytes=VMEM_LIMIT, collective_id=2, has_side_effects=True
         ),
-        out_shape=[
-            jax.ShapeDtypeStruct((rows, width), B16),
-            jax.ShapeDtypeStruct((rows, width), F32),
-            jax.ShapeDtypeStruct((rows, half), B16),
-            jax.ShapeDtypeStruct((rows, half), B16),
-            jax.ShapeDtypeStruct((2, rank, half), F32),
-            full_t, full_t, full_t, split_t, split_t,
-        ],
-        compiler_params=params(),
         cost_estimate=pl.CostEstimate(
             flops=2 * rows * width * (16 * hidden_half // 2 + 4 * half),
             bytes_accessed=40 * 2**20,
             transcendentals=rows * hidden_half * 2,
         ),
-    )(
-        side, x, cot, own, other, w_o, w_e, w_r, out_off, gain, shift, wide_off, shrink_off,
-        od, ou, ed, ru, eu, rd,
-    )
+    )(x, cot, attended, other, w_o, factors, shared, offsets, out_off, gain, shift, shrink_off, w_e, w_r)
 
 
 def unproject_body(
@@ -851,23 +1532,13 @@
         return jnp.where(tp == 0, jnp.stack([mine, others]), jnp.stack([others, mine]))
 
     mine_of = lambda array, axis=0: lax.dynamic_index_in_dim(array, tp, axis, keepdims=False)
-
-    def gather(weight):
-        whole = lax.all_gather(weight, ("shard", "tp"), axis=0, tiled=False)
-        return whole.reshape((2 * planes, 2) + weight.shape)
-
-    x = turn(mine_of(tokens))
-    w_j = gather(jnp.transpose(joined_weight, (1, 0, 2)))
-    places = turn(mine_of(positions, 1))
-    cot = turn(mine_of(cotangent))
-    w_o = gather(output_weight)
-    w_e = gather(expand_weight)
-    w_r = gather(reduce_weight)
-
-    away = to_core(adapter_pick)
-    picks = jnp.where(core == ctx, adapter_pick, away)
-    pick = lax.dynamic_index_in_dim(picks, tp, 0, keepdims=False)
-    pick_next = lax.dynamic_index_in_dim(picks, 1 - tp, 0, keepdims=False)
+    half = joined_weight.shape[2]
+    hidden_half = expand_weight.shape[1]
+    rank = joined_up.shape[1]
+    rows = tokens.shape[1]
+
+    pick = lax.dynamic_index_in_dim(adapter_pick, tp, 0, keepdims=False)
+    pick_next = lax.dynamic_index_in_dim(adapter_pick, 1 - tp, 0, keepdims=False)
 
     def row(table, at):
         return lax.dynamic_index_in_dim(table, at, 0, keepdims=False)
@@ -876,50 +1547,44 @@
         ju, od, eu, rd = row(joined_up, at), row(output_down, at), row(expand_up, at), row(reduce_down, at)
         return jnp.concatenate([ju.reshape(ju.shape[0], -1), od.T, eu, rd.T], axis=1)
 
-    packed = by_tp(split_factors(pick), to_tp(split_factors(pick_next)))
-    half = joined_weight.shape[2]
-    hidden_half = expand_weight.shape[1]
-    rank = joined_up.shape[1]
-    ju = jnp.transpose(packed[:, :, : 3 * half].reshape(2, rank, 3, half), (0, 2, 1, 3))
-    od = packed[:, :, 3 * half : 4 * half]
-    eu = packed[:, :, 4 * half : 4 * half + hidden_half]
-    rd = packed[:, :, 4 * half + hidden_half :]
-    jd, ed = row(joined_down, pick).T, row(expand_down, pick).T
-    ou, ru = row(output_up, pick), row(reduce_up, pick)
+    shared = jnp.concatenate(
+        [
+            row(joined_down, pick).T, row(expand_down, pick).T, row(output_up, pick), row(reduce_up, pick),
+            jnp.full((rank, 128), pick.astype(B16)),
+        ],
+        axis=1,
+    )
     offsets = jnp.concatenate([joined_bias.reshape(-1), widening_offset])[None]
-    offsets = by_tp(offsets, to_tp(offsets))
-    bias = offsets[:, :, : 3 * half].reshape(2, 3, 1, half)
-    wide_off = offsets[:, 0, 3 * half :].reshape(1, 2 * hidden_half)
-
-    places_all = jnp.concatenate([places, to_core(places)], axis=1).astype(F32)
+
     lane = jnp.arange(128, dtype=jnp.int32) % 64
-    within = lane % 20
-    rates = jnp.exp((within % 10).astype(F32) * (-math.log(10000.0) / 10.0))
-    spot = jnp.where(
-        lane < 20, places_all[0][:, None], jnp.where(lane < 40, places_all[1][:, None], places_all[2][:, None])
-    )
-    angle = spot * rates
-    turned = lane < 60
-    cosine = jnp.where(turned, jnp.cos(angle), 1.0)
-    sine = jnp.where(turned, jnp.where(within < 10, -jnp.sin(angle), jnp.sin(angle)), 0.0)
-    rows = x.shape[0]
-
-    *qkv, xn1, u1 = project(
-        side, x, first_gain[None], first_shift[None], w_j, bias, jd, ju, cosine[:rows], sine[:rows]
-    )
-    query, key, value = (
-        jnp.concatenate([mine, to_core(sent)], axis=0) for mine, sent in zip(qkv[:3], qkv[3:])
-    )
-    attended, inverse, weights = attend(query, key, value)
-    own_heads, other_heads = attended[:rows], to_core(attended[rows:])
-    out, gh, gown, gother, t_od, t_ou, t_ed, t_ru, t_eu, t_rd = middle(
-        side, x, cot, own_heads, other_heads, w_o, w_e, w_r,
-        mixing_exit_offset[None], second_gain[None], second_shift[None], wide_off, shrinking_offset[None],
-        od, ou, ed, ru, eu, rd,
-    )
+    rates = jnp.exp((lane % 10).astype(F32) * (-math.log(10000.0) / 10.0))
+    rates = jnp.where(lane[None] // 20 == jnp.arange(3)[:, None], rates[None], 0.0)
+    high = lax.reduce_precision(rates, 8, 7)
+    mid = lax.reduce_precision(rates - high, 8, 7)
+    low = lax.reduce_precision(rates - high - mid, 8, 7)
+    rates = jnp.concatenate([high, mid, low, jnp.zeros((7, 128), F32)], axis=0).astype(B16)
+    spots = mine_of(positions, 1).astype(B16)
+    spots = jnp.concatenate([spots, spots, spots, jnp.zeros((7, rows), B16)], axis=0)
+
+    (
+        x, factors, shared, offsets, w_j, w_o, w_e, w_r, query, key, value, xn1, u1, cosine, sine,
+    ) = project(
+        planes, tokens, spots, split_factors(pick), split_factors(pick_next), shared, offsets,
+        jnp.transpose(joined_weight, (1, 0, 2)), output_weight, expand_weight, reduce_weight,
+        first_gain[None], first_shift[None], rates,
+    )
+    attended, inverse, weights, other_heads, cot, w_o, w_e, w_r = attend(
+        planes, query, key, value, cotangent, output_weight, expand_weight, reduce_weight, w_o, w_e, w_r
+    )
+    out, gh, t_od, t_ou, t_ed, t_ru, t_eu, t_rd, grad_att, w_e, w_r = middle(
+        planes, x, cot, attended, other_heads, w_o, factors, shared, offsets,
+        mixing_exit_offset[None], second_gain[None], second_shift[None], shrinking_offset[None], w_e, w_r,
+    )
+    jd = shared[:, : tokens.shape[2]]
+    ju = jnp.transpose(factors[:, :, : 3 * half].reshape(2, rank, 3, half), (0, 2, 1, 3))
+    tag = shared[: rank // 2, -128:]
     out = turn(out)
     output = by_tp(out, to_tp(out))
-    grad_att = jnp.concatenate([gown, to_core(gother)], axis=0)
     grads = attend_back(query, key, value, attended, inverse, grad_att, weights, cosine, sine)
     tokens_part, t_fd, t_fu = unproject(
         side, x, gh, xn1, u1, first_gain[None], w_j, jd, ju,
@@ -939,7 +1604,6 @@
         send = lax.dynamic_slice_in_dim(wide, (1 - core) * low_rank, low_rank, 0)
         total = (keep + to_core(send.astype(B16)).astype(F32)).astype(B16)
         width = split_parts.shape[2]
-        tag = jnp.full((low_rank, 128), pick.astype(B16))
         rest = jnp.concatenate([total[:, 2 * width :], tag], axis=1)
         keep = jnp.concatenate([lax.dynamic_slice_in_dim(total, tp * width, width, 1), rest], axis=1)
         send = jnp.concatenate([lax.dynamic_slice_in_dim(total, (1 - tp) * width, width, 1), rest], axis=1)
@@ -992,7 +1656,7 @@
 
 def solution(mesh):
     sizes = dict(mesh.shape)
-    if sizes["ctx"] == 2 and sizes["tp"] == 2 and sizes["shard"] % 2 == 0:
+    if sizes["ctx"] == 2 and sizes["tp"] == 2 and sizes["shard"] == 8:
         body = functools.partial(clip_shards, sizes["shard"] // 2)
     else:
         body = general_shards

time: 611 us -> 515 us (0.84)
  waiting for transfers between devices: 179 us -> 70.7 us
  Pallas kernels: 243 us -> 331 us
  starting transfers between devices: 66.4 us -> 35.8 us
  local copies, waits for them, and re-layouts: 63.2 us -> 42.1 us
  between operations: 19.3 us -> 6.02 us
  other arithmetic: 24.9 us -> 15.6 us
    all_gather x4 -> x0, waiting for transfers between devices: 115 us -> none  [gather(): whole = lax.all_gather(weight, ('shard', 'tp'), axis=0, tiled=False)]
    pallas_call x3, Pallas kernels: 150 us -> 238 us  [the longest x1 90.8 us: middle(): pl.pallas_call(functools.partial(middle_body, planes, blocks), grid=(2 *...]
    ppermute x1, waiting for transfers between devices: 35.5 us -> 0.01 us  [clip_shards(): lax.ppermute(leave, ('shard', 'ctx', 'tp'), turns_flip)]
    ppermute x5 -> x3, waiting for transfers between devices: 7.74 us -> 33.1 us  [to_tp(): return lax.ppermute(array, 'tp', pair)]
    ppermute x5 -> x2, starting transfers between devices: 46.9 us -> 26.6 us  [turn(): return lax.ppermute(array, ('shard', 'ctx'), turns)]
    ppermute x6, waiting for transfers between devices: 1.31 us -> 14 us  [spread(): lax.ppermute(stack, 'shard', [(i, (i + 2 * shift) % (2 * planes)) for i i...]
    select_n x2 -> x1, other arithmetic: 9.46 us -> 0.01 us  [clip_shards(): lane[None] // 20 == jnp.arange(3)[:, None]]
    ppermute x2, waiting for transfers between devices: 15.4 us -> 23.6 us  [to_ctx(): return lax.ppermute(array, 'ctx', pair)]
  transfers between devices with their start and end apart: 37 -> 21, of which waited for: 10 -> 8; matrix products, arithmetic and copies ran while one was open for 14% -> 8% of each run, Pallas kernels for 27% -> 18%
where the time goes in v2:
time: 515 us; the launch traced here: 506 us
  Pallas kernels  331 us (64%)
  waiting for transfers between devices  70.7 us (14%)
  local copies, waits for them, and re-layouts  42.1 us (8%)
  starting transfers between devices  35.8 us (7%)
  other arithmetic  15.6 us (3%)
  between operations  6.02 us (1%)
    pallas_call x1, Pallas kernels, middle(): pl.pallas_call(functools.partial(middle_body, planes, blocks), grid=(2 *...  90.8 us
    pallas_call x1, Pallas kernels, project(): pl.pallas_call(functools.partial(project_body, planes, blocks), in_specs=...  77.1 us
    pallas_call x1, Pallas kernels, attend_back(): pl.pallas_call(attend_back_body, grid=(width // 128, length // block), in...  74.5 us
    pallas_call x1, Pallas kernels, attend(): pl.pallas_call(functools.partial(attend_body, planes, blocks), grid=(pair...  69.9 us
    ppermute x3, waiting for transfers between devices, to_tp(): return lax.ppermute(array, 'tp', pair)  33.1 us
    ppermute x2, starting transfers between devices, turn(): return lax.ppermute(array, ('shard', 'ctx'), turns)  26.6 us
    ppermute x2, waiting for transfers between devices, to_ctx(): return lax.ppermute(array, 'ctx', pair)  23.6 us
    pallas_call x1, Pallas kernels, unproject(): pl.pallas_call(unproject_body, grid_spec=pltpu.PrefetchScalarGridSpec(num...  18.4 us
  transfers between devices with their start and end apart: 21, of which 8 were waited for; matrix products, arithmetic and copies ran while one was open for 8% of the time, Pallas kernels for 18%

profile of v2, /device:TPU:0, one launch (start us, length us, event | category | flops | bytes accessed | tf_op | source)
XLA Modules:
  0.0 505.6 jit_solution(2072328529301474968)
XLA Ops:
  17.4 77.1 %shard_map.303 = (bf16[1024,1024]{1,0:T(8,128)(2,1)}, bf16[2,16,6144]{2,1,0:T(8,128)(2,1)}, bf16[16,4224]{1,0:T(8,128)(2,1)}, f32[2,1,3584]{2,1,0:T(1,128)}, bf1...) custom-call(bf16[2,1024,1024]{2,1,0:T(8,128)(2,1)} %tokens_ref.1, ...), custom_call_target="tpu_custom_call" | custom-call | flops 6442450944 | bytes 104857600 | tf_op jit(solution)/shard_map/pallas_call | solution.py:813
  94.5 69.9 %shard_map.304 = (bf16[2048,512]{1,0:T(8,128)(2,1)}, f32[2048,512]{1,0:T(8,128)}, bf16[8,2048,2048]{2,1,0:T(8,128)(2,1)}, bf16[1024,512]{1,0:T(8,128)(2,1)}, bf1...) custom-call(bf16[2048,512]{1,0:T(8,128)(2,1)} %get-tuple-element.49., ...), custom_call_target="tpu_custom_call", output_to_operand_aliasing={{5}: (7, {}), {6}: (8, {}), {7}: (9, {})} | custom-call | flops 34359738368 | bytes 67108864 | tf_op jit(solution)/shard_map/pallas_call | solution.py:1041
  164.4 90.8 %shard_map.305 = (bf16[1024,1024]{1,0:T(8,128)(2,1)}, f32[1024,1024]{1,0:T(8,128)}, f32[2,16,512]{2,1,0:T(8,128)}, f32[16,1024]{1,0:T(8,128)}, f32[16,1024]{1,0:...) custom-call(bf16[1024,1024]{1,0:T(8,128)(2,1)} %get-tuple-element.48, ...), custom_call_target="tpu_custom_call", output_to_operand_aliasing={{9}: (12, {}), {10}: (13, {})} | custom-call | flops 38654705664 | bytes 41943040 | tf_op jit(solution)/shard_map/pallas_call | solution.py:1372
  258.6 74.5 %shard_map.306 = (bf16[2048,512]{1,0:T(8,128)(2,1)}, bf16[2048,512]{1,0:T(8,128)(2,1)}, bf16[2048,512]{1,0:T(8,128)(2,1)}) custom-call(bf16[2048,512]{1,0:T(8,128)(2,1)} %get-tuple-element.49.q_ref, bf16[2048,512]{1,0:T(8,128)(2,1)} %get-tuple-element.50.k_ref, bf16[2048,512]{1,0:T(8,128)(2,1)} %get-tuple-element.51.v_ref, ...), custom_call_target="tpu_custom_call" | custom-call | flops 42949672960 | bytes 67108864 | tf_op jit(solution)/shard_map/pallas_call | solution.py:1124
  333.0 3.1 fusion.24
  340.5 17.1 %collective-permute-start = (bf16[1024,1024]{1,0:T(8,128)(2,1)}, bf16[1024,1024]{1,0:T(8,128)(2,1)}, u32[]{:S(2)}, u32[]{:S(2)}) collective-permute-start(bf16[1024,1024]{1,0:T(8,128)(2,1)} %get-tuple-element.64), channel_id=1, source_target_pairs={{0,0},{2,4},{4,2},{6,6},{8,8},{10,12},{12,10},{14,14},{16,16},{18,... | collective-permute-start | bytes 6291464 | tf_op jit(solution)/shard_map/ppermute | solution.py:1520
  361.4 4.9 collective-permute-done.15
  366.4 7.5 %collective-permute-done.16 = bf16[2,8,7808]{2,1,0:T(8,128)(2,1)S(1)} collective-permute-done((bf16[2,8,7808]{2,1,0:T(8,128)(2,1)S(1)}, bf16[2,8,7808]{2,1,0:T(8,128)(2,1)S(1)}, u32[]{:S(2)}, u32[]{:S(2)}) %collective-permute-start.16) | collective-permute-done | bytes 249888 | tf_op jit(solution)/shard_map/ppermute | solution.py:1529
  374.1 1.7 collective-permute-start.18
  375.8 2.2 collective-permute-start.19
  378.0 18.4 %shard_map.307 = (bf16[1024,1024]{1,0:T(8,128)(2,1)}, f32[16,1024]{1,0:T(8,128)}, f32[2,3,16,512]{3,2,1,0:T(8,128)}) custom-call(s32[1]{0:T(128)} %bitcast.28.side, bf16[1024,1024]{1,0:T(8,128)(2,1)} %get-tuple-element.48.x_ref, f32[1024,1024]{1,0:T(8,128)} %get-tuple-element.65.gh_ref, bf16[1024,1024]{1,0:T(8,128)(2,1)} %get-tuple-element.66.xn_ref, ...), custom_call_target="tpu_custom_call" | custom-call | flops 6442450944 | bytes 20971520 | tf_op jit(solution)/shard_map/pallas_call | solution.py:1456
  398.6 3.0 constant_dynamic-slice_fusion.5
  401.7 9.5 %collective-permute-start.5 = (bf16[512,1024]{1,0:T(8,128)(2,1)}, bf16[512,1024]{1,0:T(8,128)(2,1)}, u32[]{:S(2)}, u32[]{:S(2)}) collective-permute-start(bf16[512,1024]{1,0:T(8,128)(2,1)} %get-tuple-element.121), channel_id=1, source_target_pairs={{0,0},{2,4},{4,2},{6,6},{8,8},{10,12},{12,10},{14,14},{16,16},{18,... | collective-permute-start | bytes 3145736 | tf_op jit(solution)/shard_map/ppermute | solution.py:1520
  412.4 2.9 collective-permute-done.8
  415.7 16.1 %collective-permute-done.9 = bf16[2,8,2688]{2,0,1:T(2,128)(2,1)S(1)} collective-permute-done((bf16[2,8,2688]{2,0,1:T(2,128)(2,1)S(1)}, bf16[2,8,2688]{2,0,1:T(2,128)(2,1)S(1)}, u32[]{:S(2)}, u32[]{:S(2)}) %collective-permute-start.9) | collective-permute-done | bytes 86048 | tf_op jit(solution)/shard_map/ppermute | solution.py:1529
  434.2 5.2 %collective-permute-done.10 = bf16[4,8,2688]{2,0,1:T(4,128)(2,1)S(1)} collective-permute-done((bf16[4,8,2688]{2,0,1:T(4,128)(2,1)S(1)}, bf16[4,8,2688]{2,0,1:T(4,128)(2,1)S(1)}, u32[]{:S(2)}, u32[]{:S(2)}) %collective-permute-start.10) | collective-permute-done | bytes 172064 | tf_op jit(solution)/shard_map/ppermute | solution.py:1615
  439.5 4.8 collective-permute-done.11
  446.0 4.0 collective-permute-done.12
  449.9 2.6 concatenate.84
  452.7 3.9 maximum_select_fusion.2
  460.0 2.9 maximum_select_fusion.1
  463.5 4.3 fusion
  475.5 25.4 %collective-permute-done.1 = bf16[1024,1024]{1,0:T(8,128)(2,1)S(1)} collective-permute-done((bf16[1024,1024]{1,0:T(8,128)(2,1)}, bf16[1024,1024]{1,0:T(8,128)(2,1)S(1)}, u32[]{:S(2)}, u32[]{:S(2)}) %collective-permute-start.1) | collective-permute-done | bytes 2097184 | tf_op jit(solution)/shard_map/ppermute | solution.py:1526
  500.9 4.5 maximum_select_fusion
  (134 shorter events, 43.3 us)
Async XLA Ops:
  0.6 10.2 %copy-start = (s32[3,2,1024]{2,1,0:T(2,128)S(1)}, s32[3,2,1024]{2,1,0:T(2,128)}, u32[]{:S(2)}) copy-start(s32[3,2,1024]{2,1,0:T(2,128)} %param.27) | copy-start | bytes 73732
  258.3 102.9 %collective-permute-start.14 = (bf16[8,12288]{1,0:T(8,128)(2,1)S(1)}, bf16[8,12288]{1,0:T(8,128)(2,1)S(1)}, u32[]{:S(2)}, u32[]{:S(2)}) collective-permute-start(bf16[8,12288]{1,0:T(8,128)(2,1)S(1)} %dynamic-slice_convert_fusion), channel_id=1, source_target_pairs={{0,4},{4,0},{8,12},{12,8},{16,20},{20,16},{24,28},{28,24},{1,5},{5... | collective-permute-start | bytes 589832 | tf_op jit(solution)/shard_map/ppermute | solution.py:1523
  333.0 3.5 copy-start.3
  336.2 37.9 %collective-permute-start.2 = (bf16[1024,512]{1,0:T(8,128)(2,1)}, bf16[1024,512]{1,0:T(8,128)(2,1)}, u32[]{:S(2)}, u32[]{:S(2)}) collective-permute-start(bf16[1024,512]{1,0:T(8,128)(2,1)} %get-tuple-element.127), channel_id=1, source_target_pairs={{0,4},{4,0},{8,12},{12,8},{16,20},{20,16},{24,28},{28,24},{1,5},{5... | collective-permute-start | bytes 3145736 | tf_op jit(solution)/shard_map/ppermute | solution.py:1523
  338.0 37.9 %collective-permute-start.3 = (bf16[1024,512]{1,0:T(8,128)(2,1)}, bf16[1024,512]{1,0:T(8,128)(2,1)}, u32[]{:S(2)}, u32[]{:S(2)}) collective-permute-start(bf16[1024,512]{1,0:T(8,128)(2,1)} %get-tuple-element.125), channel_id=1, source_target_pairs={{0,4},{4,0},{8,12},{12,8},{16,20},{20,16},{24,28},{28,24},{1,5},{5... | collective-permute-start | bytes 3145736 | tf_op jit(solution)/shard_map/ppermute | solution.py:1523
  340.3 37.7 %collective-permute-start.4 = (bf16[1024,512]{1,0:T(8,128)(2,1)}, bf16[1024,512]{1,0:T(8,128)(2,1)}, u32[]{:S(2)}, u32[]{:S(2)}) collective-permute-start(bf16[1024,512]{1,0:T(8,128)(2,1)} %get-tuple-element.123), channel_id=1, source_target_pairs={{0,4},{4,0},{8,12},{12,8},{16,20},{20,16},{24,28},{28,24},{1,5},{5... | collective-permute-start | bytes 3145736 | tf_op jit(solution)/shard_map/ppermute | solution.py:1523
  340.5 112.1 %collective-permute-start = (bf16[1024,1024]{1,0:T(8,128)(2,1)}, bf16[1024,1024]{1,0:T(8,128)(2,1)}, u32[]{:S(2)}, u32[]{:S(2)}) collective-permute-start(bf16[1024,1024]{1,0:T(8,128)(2,1)} %get-tuple-element.64), channel_id=1, source_target_pairs={{0,0},{2,4},{4,2},{6,6},{8,8},{10,12},{12,10},{14,14},{16,16},{18,... | collective-permute-start | bytes 6291464 | tf_op jit(solution)/shard_map/ppermute | solution.py:1520
  361.3 5.0 collective-permute-start.15
  366.3 7.6 %collective-permute-start.16 = (bf16[2,8,7808]{2,1,0:T(8,128)(2,1)S(1)}, bf16[2,8,7808]{2,1,0:T(8,128)(2,1)S(1)}, u32[]{:S(2)}, u32[]{:S(2)}) collective-permute-start(bf16[2,8,7808]{2,1,0:T(8,128)(2,1)S(1)} %pad_maximum_fusion.1), channel_id=1, source_target_pairs={{0,2},{2,0},{1,3},{3,1},{4,6},{6,4},{5,7},{7,5},{8,10},{10,8},{9,1... | collective-permute-start | bytes 749576 | tf_op jit(solution)/shard_map/ppermute | solution.py:1529
  374.0 37.2 %collective-permute-start.17 = (bf16[4,8,7808]{2,1,0:T(8,128)(2,1)S(1)}, bf16[4,8,7808]{2,1,0:T(8,128)(2,1)}, u32[]{:S(2)}, u32[]{:S(2)}) collective-permute-start(bf16[4,8,7808]{2,1,0:T(8,128)(2,1)S(1)} %pad_maximum_fusion), channel_id=1, source_target_pairs={{0,8},{4,12},{8,16},{12,20},{16,24},{20,28},{24,0},{28,4},{1,9},{5... | collective-permute-start | bytes 1499144 | tf_op jit(solution)/shard_map/ppermute | solution.py:1615
  374.1 41.5 %collective-permute-start.18 = (bf16[4,8,7808]{2,1,0:T(8,128)(2,1)S(1)}, bf16[4,8,7808]{2,1,0:T(8,128)(2,1)S(1)}, u32[]{:S(2)}, u32[]{:S(2)}) collective-permute-start(bf16[4,8,7808]{2,1,0:T(8,128)(2,1)S(1)} %pad_maximum_fusion), channel_id=1, source_target_pairs={{0,16},{4,20},{8,24},{12,28},{16,0},{20,4},{24,8},{28,12},{1,17},{... | collective-permute-start | bytes 1499144 | tf_op jit(solution)/shard_map/ppermute | solution.py:1615
  375.8 56.8 %collective-permute-start.19 = (bf16[4,8,7808]{2,1,0:T(8,128)(2,1)S(1)}, bf16[4,8,7808]{2,1,0:T(8,128)(2,1)S(1)}, u32[]{:S(2)}, u32[]{:S(2)}) collective-permute-start(bf16[4,8,7808]{2,1,0:T(8,128)(2,1)S(1)} %pad_maximum_fusion), channel_id=1, source_target_pairs={{0,24},{4,28},{8,0},{12,4},{16,8},{20,12},{24,16},{28,20},{1,25},{... | collective-permute-start | bytes 1499144 | tf_op jit(solution)/shard_map/ppermute | solution.py:1615
  398.6 3.1 collective-permute-start.7
  401.7 51.0 %collective-permute-start.5 = (bf16[512,1024]{1,0:T(8,128)(2,1)}, bf16[512,1024]{1,0:T(8,128)(2,1)}, u32[]{:S(2)}, u32[]{:S(2)}) collective-permute-start(bf16[512,1024]{1,0:T(8,128)(2,1)} %get-tuple-element.121), channel_id=1, source_target_pairs={{0,0},{2,4},{4,2},{6,6},{8,8},{10,12},{12,10},{14,14},{16,16},{18,... | collective-permute-start | bytes 3145736 | tf_op jit(solution)/shard_map/ppermute | solution.py:1520
  411.2 4.1 collective-permute-start.8
  415.3 37.4 %collective-permute-start.6 = (bf16[512,1024]{1,0:T(8,128)(2,1)}, bf16[512,1024]{1,0:T(8,128)(2,1)}, u32[]{:S(2)}, u32[]{:S(2)}) collective-permute-start(bf16[512,1024]{1,0:T(8,128)(2,1)} %get-tuple-element.122), channel_id=1, source_target_pairs={{0,1},{1,0},{2,5},{3,4},{4,3},{5,2},{6,7},{7,6},{8,9},{9,8},{10,13... | collective-permute-start | bytes 3145736 | tf_op jit(solution)/shard_map/ppermute | solution.py:1596
  415.6 16.2 %collective-permute-start.9 = (bf16[2,8,2688]{2,0,1:T(2,128)(2,1)S(1)}, bf16[2,8,2688]{2,0,1:T(2,128)(2,1)S(1)}, u32[]{:S(2)}, u32[]{:S(2)}) collective-permute-start(bf16[2,8,2688]{2,0,1:T(2,128)(2,1)S(1)} %pad_maximum_fusion.9), channel_id=1, source_target_pairs={{0,2},{2,0},{1,3},{3,1},{4,6},{6,4},{5,7},{7,5},{8,10},{10,8},{9,1... | collective-permute-start | bytes 258056 | tf_op jit(solution)/shard_map/ppermute | solution.py:1529
  432.1 7.4 %collective-permute-start.10 = (bf16[4,8,2688]{2,0,1:T(4,128)(2,1)S(1)}, bf16[4,8,2688]{2,0,1:T(4,128)(2,1)S(1)}, u32[]{:S(2)}, u32[]{:S(2)}) collective-permute-start(bf16[4,8,2688]{2,0,1:T(4,128)(2,1)S(1)} %pad_maximum_fusion.4), channel_id=1, source_target_pairs={{0,8},{4,12},{8,16},{12,20},{16,24},{20,28},{24,0},{28,4},{1,9},{5... | collective-permute-start | bytes 516104 | tf_op jit(solution)/shard_map/ppermute | solution.py:1615
  432.7 11.6 %collective-permute-start.11 = (bf16[4,8,2688]{2,0,1:T(4,128)(2,1)S(1)}, bf16[4,8,2688]{2,0,1:T(4,128)(2,1)S(1)}, u32[]{:S(2)}, u32[]{:S(2)}) collective-permute-start(bf16[4,8,2688]{2,0,1:T(4,128)(2,1)S(1)} %pad_maximum_fusion.4), channel_id=1, source_target_pairs={{0,16},{4,20},{8,24},{12,28},{16,0},{20,4},{24,8},{28,12},{1,17},{... | collective-permute-start | bytes 516104 | tf_op jit(solution)/shard_map/ppermute | solution.py:1615
  439.5 20.5 %collective-permute-start.20 = (bf16[16,8,7808]{2,1,0:T(8,128)(2,1)S(1)}, bf16[16,8,7808]{2,1,0:T(8,128)(2,1)}, u32[]{:S(2)}, u32[]{:S(2)}) collective-permute-start(bf16[16,8,7808]{2,1,0:T(8,128)(2,1)S(1)} %constant_dynamic-update-slice_fusion.14), channel_id=1, source_target_pairs={{0,4},{4,0},{8,12},{12,8},{16,20},{20,16},{24,28},{28,24},{1,5},{5... | collective-permute-start | bytes 5996552 | tf_op jit(solution)/shard_map/ppermute | solution.py:1523
  444.2 5.7 %collective-permute-start.12 = (bf16[4,8,2688]{2,0,1:T(4,128)(2,1)S(1)}, bf16[4,8,2688]{2,0,1:T(4,128)(2,1)}, u32[]{:S(2)}, u32[]{:S(2)}) collective-permute-start(bf16[4,8,2688]{2,0,1:T(4,128)(2,1)S(1)} %pad_maximum_fusion.4), channel_id=1, source_target_pairs={{0,24},{4,28},{8,0},{12,4},{16,8},{20,12},{24,16},{28,20},{1,25},{... | collective-permute-start | bytes 516104 | tf_op jit(solution)/shard_map/ppermute | solution.py:1615
  452.5 4.1 collective-permute-start.13
  452.6 48.2 %collective-permute-start.1 = (bf16[1024,1024]{1,0:T(8,128)(2,1)}, bf16[1024,1024]{1,0:T(8,128)(2,1)S(1)}, u32[]{:S(2)}, u32[]{:S(2)}) collective-permute-start(bf16[1024,1024]{1,0:T(8,128)(2,1)} %collective-permute-done), channel_id=1, source_target_pairs={{0,1},{1,0},{2,3},{3,2},{4,5},{5,4},{6,7},{7,6},{8,9},{9,8},{10,11... | collective-permute-start | bytes 6291464 | tf_op jit(solution)/shard_map/ppermute | solution.py:1526
  500.9 4.5 copy-start.1
  (5 other events, 12.0 us)
